TPU v7x, 512 devices: a whole 4x8x8 slice. The times are simulated.
512 devices in a mesh: rep: 16 (over x, y_lo, core), fsdp: 32 (over z, y_hi).
Axes of the slice: x: 4, y: 8 (y_hi: 4, y_lo: 2; y = y_hi * 2 + y_lo), z: 8, core: 2. Of those that a mesh axis runs over, the one named last changes fastest.
Arguments:
- gradient: bfloat16 [1024, 32768], P('fsdp', 'rep'), may hold values from -6 to 6
- owner_table: int32 [16, 2], replicated, may hold values from 0 to 1, each once within a row
- left_factor: float32 [16, 2048, 1024], P('rep', 'fsdp'), may hold values from -1 to 5
- right_factor: float32 [16, 2048, 1024], P('rep', 'fsdp'), may hold values from -1 to 5
- left_root: bfloat16 [16, 2048, 1024], P('rep', 'fsdp'), may hold values from -1 to 5, as said below
- right_root: bfloat16 [16, 2048, 1024], P('rep', 'fsdp'), may hold values from -1 to 5, as said below
Outputs:
- update: bfloat16 [1024, 32768], P('fsdp')
- left_new: float32 [16, 2048, 1024], P('rep', 'fsdp')
- right_new: float32 [16, 2048, 1024], P('rep', 'fsdp')
Inputs may be any that keep to these rules, and one draw needn't show every extreme that they name: `owner_table`: each row is a permutation of the groups. `left_root`: each 1024 x 1024 block of a group is symmetric. `right_root`: each 1024 x 1024 block of a group is symmetric.
All inputs are finite; a program needn't handle non-finite values.
Results may differ from a plain program's by a relative error of at most 0.005.
Values may be sent and summed in bfloat16 or wider, within the bound.
A program may use at most 64 MiB of HBM per device.

v0:
```python
import jax
import jax.numpy as jnp
from jax import lax
from jax.sharding import PartitionSpec as P

BETA = 0.9
EPSILON = 1e-06


def swapped(x, axis, distance):
    return lax.ppermute(x, axis, [(i, i ^ 1 << distance) for i in range(lax.axis_size(axis))])


def paired(mine, other, lower, axis):
    first = jnp.where(lower, mine, other)
    second = jnp.where(lower, other, mine)
    return jnp.concatenate([first, second], axis=axis)


def body(gradient, owner_table, left_factor, right_factor, left_root, right_root):
    width = left_factor.shape[2]
    quarter = left_factor.shape[1]
    members = width // quarter
    levels = members.bit_length() - 1
    shard_rows = gradient.shape[0]
    groups = owner_table.shape[1]
    fsdp_index = lax.axis_index("fsdp")
    member = fsdp_index % members
    replica = lax.axis_index("rep")
    own_order = lax.dynamic_slice_in_dim(owner_table, replica, 1, 0)[0]
    positions = jnp.arange(groups, dtype=jnp.int32)
    match = own_order[None, :] == positions[:, None]
    inverse = jnp.sum(jnp.where(match, positions[None, :], 0), axis=1)
    slab = gradient.reshape(shard_rows, groups, width)
    ordered = jnp.take(slab, inverse, axis=1)
    own_columns = lax.all_to_all(
        ordered.reshape(shard_rows, groups * width), "fsdp", split_axis=1, concat_axis=0, tiled=True
    )
    block = own_columns
    for bit in range(levels):
        lower = fsdp_index >> bit & 1 == 0
        other = swapped(block, "fsdp", bit)
        block = paired(block, other, lower, 1)
    own_rows = lax.dynamic_slice_in_dim(block, member * quarter, quarter, 0)
    left_stat = lax.dot_general(
        own_rows, block, (((1,), (1,)), ((), ())), preferred_element_type=jnp.float32
    )
    right_stat = lax.dot_general(
        own_columns, block, (((0,), (0,)), ((), ())), preferred_element_type=jnp.float32
    )
    left_new = BETA * left_factor[0] + (1.0 - BETA) / width * left_stat
    right_new = BETA * right_factor[0] + (1.0 - BETA) / width * right_stat
    products = jnp.dot(left_root[0], block, preferred_element_type=jnp.float32).astype(jnp.bfloat16)
    for bit in range(levels):
        lower = fsdp_index >> bit & 1 == 0
        other = swapped(products, "fsdp", bit)
        products = paired(products, other, lower, 0)
    precond = lax.dot_general(
        products, right_root[0], (((1,), (1,)), ((), ())), preferred_element_type=jnp.float32
    )
    squares = jnp.sum(precond * precond)
    for bit in range(levels):
        squares = squares + swapped(squares, "fsdp", bit)
    block_float = block.astype(jnp.float32)
    grad_squares = jnp.sum(block_float * block_float)
    scaled = (precond * (jnp.sqrt(grad_squares) / jnp.sqrt(squares + EPSILON))).astype(jnp.bfloat16)
    arrived = lax.all_to_all(scaled, "fsdp", split_axis=0, concat_axis=1, tiled=True)
    arranged = arrived.reshape(shard_rows, groups, width)
    placed = jnp.take(arranged, own_order, axis=1)
    update = lax.all_gather(placed.reshape(shard_rows, groups * width), "rep", axis=1, tiled=True)
    return (update, left_new[None], right_new[None])


def solution(mesh):
    placed = (
        P("fsdp", "rep"),
        P(),
        P("rep", "fsdp", None),
        P("rep", "fsdp", None),
        P("rep", "fsdp", None),
        P("rep", "fsdp", None),
    )
    return jax.shard_map(
        body,
        mesh=mesh,
        in_specs=placed,
        out_specs=(P("fsdp", None), P("rep", "fsdp", None), P("rep", "fsdp", None)),
        check_vma=False,
    )
```

profile of v0, /device:TPU:1, one launch (start us, length us, event | category | flops | bytes accessed | tf_op | source)
XLA Modules:
  0.0 329.9 jit_solution(10194362096943727050)
XLA Ops:
  7.2 0.9 dynamic-slice_reduce_fusion
  8.2 0.9 copy.37
  9.2 0.6 gather_fusion
  10.0 0.2 all_to_all.26
  10.5 27.6 %all_to_all.35 = bf16[32,2,1024]{2,1,0:T(2,128)(2,1)S(1)} all-to-all(bf16[32,2,1024]{2,1,0:T(2,128)(2,1)S(1)} %reshape.59), channel_id=1, replica_groups=mesh['rep'=16,'fsdp'=32] {'fsdp'}, dimensions={0} | all-to-all | bytes 262144 | tf_op jit(solution)/shard_map/all_to_all | solution.py:36
  38.1 0.2 reshape.60
  38.4 2.3 collective-permute-start
  40.7 14.2 %collective-permute-done = bf16[1024,64]{1,0:T(8,128)(2,1)S(1)} collective-permute-done((bf16[1024,64]{1,0:T(8,128)(2,1)S(1)}, bf16[1024,64]{1,0:T(8,128)(2,1)S(1)}, u32[]{:S(2)}, u32[]{:S(2)}) %collective-permute-start) | collective-permute-done | bytes 131104 | tf_op jit(solution)/shard_map/ppermute | solution.py:11
  55.1 3.1 collective-permute-start.1
  58.1 14.6 %collective-permute-done.1 = bf16[1024,128]{1,0:T(8,128)(2,1)S(1)} collective-permute-done((bf16[1024,128]{1,0:T(8,128)(2,1)S(1)}, bf16[1024,128]{1,0:T(8,128)(2,1)S(1)}, u32[]{:S(2)}, u32[]{:S(2)}) %collective-permute-start.1) | collective-permute-done | bytes 262176 | tf_op jit(solution)/shard_map/ppermute | solution.py:11
  72.7 0.2 broadcast_select_fusion.11
  73.0 2.4 collective-permute-start.2
  75.5 12.4 %collective-permute-done.2 = bf16[1024,256]{1,0:T(8,128)(2,1)S(1)} collective-permute-done((bf16[1024,256]{1,0:T(8,128)(2,1)S(1)}, bf16[1024,256]{1,0:T(8,128)(2,1)S(1)}, u32[]{:S(2)}, u32[]{:S(2)}) %collective-permute-start.2) | collective-permute-done | bytes 524320 | tf_op jit(solution)/shard_map/ppermute | solution.py:11
  88.2 1.9 collective-permute-start.3
  90.1 48.4 %collective-permute-done.3 = bf16[1024,512]{1,0:T(8,128)(2,1)} collective-permute-done((bf16[1024,512]{1,0:T(8,128)(2,1)S(1)}, bf16[1024,512]{1,0:T(8,128)(2,1)}, u32[]{:S(2)}, u32[]{:S(2)}) %collective-permute-start.3) | collective-permute-done | bytes 1048608 | tf_op jit(solution)/shard_map/ppermute | solution.py:11
  138.5 1.6 broadcast_select_fusion.1
  140.2 0.5 fusion.8
  140.6 1.9 collective-permute-start.4
  142.6 7.0 %collective-permute-done.4 = bf16[64,1024]{1,0:T(8,128)(2,1)S(1)} collective-permute-done((bf16[64,1024]{1,0:T(8,128)(2,1)S(1)}, bf16[64,1024]{1,0:T(8,128)(2,1)S(1)}, u32[]{:S(2)}, u32[]{:S(2)}) %collective-permute-start.4) | collective-permute-done | bytes 131104 | tf_op jit(solution)/shard_map/ppermute | solution.py:11
  149.6 3.4 %collective-permute-start.5 = (bf16[128,1024]{1,0:T(8,128)(2,1)S(1)}, bf16[128,1024]{1,0:T(8,128)(2,1)S(1)}, u32[]{:S(2)}, u32[]{:S(2)}) collective-permute-start(bf16[128,1024]{1,0:T(8,128)(2,1)S(1)} %pad_maximum_fusion.6), channel_id=1, source_target_pairs={{0,2},{1,3},{2,0},{3,1},{4,6},{5,7},{6,4},{7,5},{8,10},{9,11},{10,... | collective-permute-start | bytes 786440 | tf_op jit(solution)/shard_map/ppermute | solution.py:11
  153.1 14.6 %collective-permute-done.5 = bf16[128,1024]{1,0:T(8,128)(2,1)S(1)} collective-permute-done((bf16[128,1024]{1,0:T(8,128)(2,1)S(1)}, bf16[128,1024]{1,0:T(8,128)(2,1)S(1)}, u32[]{:S(2)}, u32[]{:S(2)}) %collective-permute-start.5) | collective-permute-done | bytes 262176 | tf_op jit(solution)/shard_map/ppermute | solution.py:11
  167.9 1.9 collective-permute-start.6
  169.8 13.0 %collective-permute-done.6 = bf16[256,1024]{1,0:T(8,128)(2,1)S(1)} collective-permute-done((bf16[256,1024]{1,0:T(8,128)(2,1)S(1)}, bf16[256,1024]{1,0:T(8,128)(2,1)S(1)}, u32[]{:S(2)}, u32[]{:S(2)}) %collective-permute-start.6) | collective-permute-done | bytes 524320 | tf_op jit(solution)/shard_map/ppermute | solution.py:11
  182.8 0.3 broadcast_select_fusion.7
  183.0 1.0 pad_maximum_fusion.2
  184.1 1.9 collective-permute-start.7
  186.0 1.7 multiply_reduce_fusion
  188.4 46.3 %collective-permute-done.7 = bf16[512,1024]{1,0:T(8,128)(2,1)} collective-permute-done((bf16[512,1024]{1,0:T(8,128)(2,1)}, bf16[512,1024]{1,0:T(8,128)(2,1)}, u32[]{:S(2)}, u32[]{:S(2)}) %collective-permute-start.7) | collective-permute-done | bytes 1048608 | tf_op jit(solution)/shard_map/ppermute | solution.py:11
  234.7 1.8 broadcast_select_fusion.3
  236.5 1.4 multiply_reduce_fusion.1
  237.8 2.0 collective-permute-start.8
  239.9 3.3 %collective-permute-done.8 = f32[]{:T(128)} collective-permute-done((f32[]{:T(128)}, f32[]{:T(128)}, u32[]{:S(2)}, u32[]{:S(2)}) %collective-permute-start.8) | collective-permute-done | bytes 36 | tf_op jit(solution)/shard_map/ppermute | solution.py:11
  244.4 4.2 %collective-permute-start.9 = (f32[]{:T(128)}, f32[]{:T(128)}, u32[]{:S(2)}, u32[]{:S(2)}) collective-permute-start(f32[]{:T(128)} %add.35), channel_id=1, source_target_pairs={{0,2},{1,3},{2,0},{3,1},{4,6},{5,7},{6,4},{7,5},{8,10},{9,11},{10,... | collective-permute-start | bytes 20 | tf_op jit(solution)/shard_map/ppermute | solution.py:11
  248.7 3.9 %collective-permute-done.9 = f32[]{:T(128)} collective-permute-done((f32[]{:T(128)}, f32[]{:T(128)}, u32[]{:S(2)}, u32[]{:S(2)}) %collective-permute-start.9) | collective-permute-done | bytes 36 | tf_op jit(solution)/shard_map/ppermute | solution.py:11
  253.2 2.6 collective-permute-start.10
  255.8 1.6 collective-permute-done.10
  258.0 2.6 collective-permute-start.11
  260.6 2.5 collective-permute-done.11
  263.9 0.9 reshape.61
  264.8 3.9 %all-to-all-start.1 = ((bf16[32,2,1024]{2,1,0:T(2,128)(2,1)}), bf16[32,2,1024]{2,1,0:T(2,128)(2,1)S(1)}, u32[]{:S(2)}, u32[]{:S(2)}) async-start(bf16[32,2,1024]{2,1,0:T(2,128)(2,1)} %reshape.61), calls=%async_computation.1 | async-start | bytes 262144 | tf_op jit(solution)/shard_map/all_to_all | solution.py:67
  268.7 11.2 %all-to-all-done.1 = bf16[32,2,1024]{2,1,0:T(2,128)(2,1)S(1)} async-done(((bf16[32,2,1024]{2,1,0:T(2,128)(2,1)}), bf16[32,2,1024]{2,1,0:T(2,128)(2,1)S(1)}, u32[]{:S(2)}, u32[]{:S(2)}) %all-to-all-start.1) | async-done | bytes 131104 | tf_op jit(solution)/shard_map/all_to_all | solution.py:67
  279.8 0.2 reshape.62
  280.4 0.6 gather_fusion.1
  281.1 0.7 copy.34
  281.8 1.2 fusion.5
  283.0 1.5 fusion.7
  284.5 35.5 %all-gather.2.cloned.1.call-done = bf16[32,32768]{1,0:T(8,128)(2,1)} async-done(((bf16[32,2048]{1,0:T(8,128)(2,1)}), bf16[32,32768]{1,0:T(8,128)(2,1)}) %all-gather.2.cloned.1.call-update) | async-done | bytes 2097168 | tf_op jit(solution)/shard_map/all_gather | solution.py:70
  320.0 3.0 copy.40
  (34 shorter events, 2.1 us)
Async XLA Ops:
  7.2 229.3 %copy-start = (bf16[1,64,1024]{2,1,0:T(8,128)(2,1)S(1)}, bf16[1,64,1024]{2,1,0:T(8,128)(2,1)}, u32[]{:S(2)}) copy-start(bf16[1,64,1024]{2,1,0:T(8,128)(2,1)} %param.13) | copy-start | bytes 393220
  38.4 16.5 %collective-permute-start = (bf16[1024,64]{1,0:T(8,128)(2,1)S(1)}, bf16[1024,64]{1,0:T(8,128)(2,1)S(1)}, u32[]{:S(2)}, u32[]{:S(2)}) collective-permute-start(bf16[1024,64]{1,0:T(8,128)(2,1)S(1)} %bitcast.43), channel_id=1, source_target_pairs={{0,1},{1,0},{2,3},{3,2},{4,5},{5,4},{6,7},{7,6},{8,9},{9,8},{10,11... | collective-permute-start | bytes 393224 | tf_op jit(solution)/shard_map/ppermute | solution.py:11
  55.1 17.7 %collective-permute-start.1 = (bf16[1024,128]{1,0:T(8,128)(2,1)S(1)}, bf16[1024,128]{1,0:T(8,128)(2,1)S(1)}, u32[]{:S(2)}, u32[]{:S(2)}) collective-permute-start(bf16[1024,128]{1,0:T(8,128)(2,1)S(1)} %pad_maximum_fusion.5), channel_id=1, source_target_pairs={{0,2},{1,3},{2,0},{3,1},{4,6},{5,7},{6,4},{7,5},{8,10},{9,11},{10,... | collective-permute-start | bytes 786440 | tf_op jit(solution)/shard_map/ppermute | solution.py:11
  73.0 14.8 %collective-permute-start.2 = (bf16[1024,256]{1,0:T(8,128)(2,1)S(1)}, bf16[1024,256]{1,0:T(8,128)(2,1)S(1)}, u32[]{:S(2)}, u32[]{:S(2)}) collective-permute-start(bf16[1024,256]{1,0:T(8,128)(2,1)S(1)} %pad_maximum_fusion.3), channel_id=1, source_target_pairs={{0,4},{1,5},{2,6},{3,7},{4,0},{5,1},{6,2},{7,3},{8,12},{9,13},{10,... | collective-permute-start | bytes 1572872 | tf_op jit(solution)/shard_map/ppermute | solution.py:11
  88.2 50.4 %collective-permute-start.3 = (bf16[1024,512]{1,0:T(8,128)(2,1)S(1)}, bf16[1024,512]{1,0:T(8,128)(2,1)}, u32[]{:S(2)}, u32[]{:S(2)}) collective-permute-start(bf16[1024,512]{1,0:T(8,128)(2,1)S(1)} %pad_maximum_fusion.1), channel_id=1, source_target_pairs={{0,8},{1,9},{2,10},{3,11},{4,12},{5,13},{6,14},{7,15},{8,0},{9,1},... | collective-permute-start | bytes 3145736 | tf_op jit(solution)/shard_map/ppermute | solution.py:11
  90.1 50.1 %copy-start.3 = (bf16[1,64,1024]{2,1,0:T(8,128)(2,1)S(1)}, bf16[1,64,1024]{2,1,0:T(8,128)(2,1)}, u32[]{:S(2)}) copy-start(bf16[1,64,1024]{2,1,0:T(8,128)(2,1)} %param.12) | copy-start | bytes 393220
  140.6 8.9 %collective-permute-start.4 = (bf16[64,1024]{1,0:T(8,128)(2,1)S(1)}, bf16[64,1024]{1,0:T(8,128)(2,1)S(1)}, u32[]{:S(2)}, u32[]{:S(2)}) collective-permute-start(bf16[64,1024]{1,0:T(8,128)(2,1)S(1)} %fusion.8), channel_id=1, source_target_pairs={{0,1},{1,0},{2,3},{3,2},{4,5},{5,4},{6,7},{7,6},{8,9},{9,8},{10,11... | collective-permute-start | bytes 393224 | tf_op jit(solution)/shard_map/ppermute | solution.py:11
  149.6 18.1 %collective-permute-start.5 = (bf16[128,1024]{1,0:T(8,128)(2,1)S(1)}, bf16[128,1024]{1,0:T(8,128)(2,1)S(1)}, u32[]{:S(2)}, u32[]{:S(2)}) collective-permute-start(bf16[128,1024]{1,0:T(8,128)(2,1)S(1)} %pad_maximum_fusion.6), channel_id=1, source_target_pairs={{0,2},{1,3},{2,0},{3,1},{4,6},{5,7},{6,4},{7,5},{8,10},{9,11},{10,... | collective-permute-start | bytes 786440 | tf_op jit(solution)/shard_map/ppermute | solution.py:11
  167.9 14.9 %collective-permute-start.6 = (bf16[256,1024]{1,0:T(8,128)(2,1)S(1)}, bf16[256,1024]{1,0:T(8,128)(2,1)S(1)}, u32[]{:S(2)}, u32[]{:S(2)}) collective-permute-start(bf16[256,1024]{1,0:T(8,128)(2,1)S(1)} %pad_maximum_fusion.4), channel_id=1, source_target_pairs={{0,4},{1,5},{2,6},{3,7},{4,0},{5,1},{6,2},{7,3},{8,12},{9,13},{10,... | collective-permute-start | bytes 1572872 | tf_op jit(solution)/shard_map/ppermute | solution.py:11
  184.1 50.6 %collective-permute-start.7 = (bf16[512,1024]{1,0:T(8,128)(2,1)}, bf16[512,1024]{1,0:T(8,128)(2,1)}, u32[]{:S(2)}, u32[]{:S(2)}) collective-permute-start(bf16[512,1024]{1,0:T(8,128)(2,1)} %pad_maximum_fusion.2), channel_id=1, source_target_pairs={{0,8},{1,9},{2,10},{3,11},{4,12},{5,13},{6,14},{7,15},{8,0},{9,1},... | collective-permute-start | bytes 3145736 | tf_op jit(solution)/shard_map/ppermute | solution.py:11
  237.8 43.9 %copy-start.2 = (f32[1,64,1024]{2,1,0:T(8,128)S(1)}, f32[1,64,1024]{2,1,0:T(8,128)}, u32[]{:S(2)}) copy-start(f32[1,64,1024]{2,1,0:T(8,128)} %param.11) | copy-start | bytes 786436
  237.8 5.4 %collective-permute-start.8 = (f32[]{:T(128)}, f32[]{:T(128)}, u32[]{:S(2)}, u32[]{:S(2)}) collective-permute-start(f32[]{:T(128)} %get-tuple-element.20), channel_id=1, source_target_pairs={{0,1},{1,0},{2,3},{3,2},{4,5},{5,4},{6,7},{7,6},{8,9},{9,8},{10,11... | collective-permute-start | bytes 20 | tf_op jit(solution)/shard_map/ppermute | solution.py:11
  244.4 8.1 %collective-permute-start.9 = (f32[]{:T(128)}, f32[]{:T(128)}, u32[]{:S(2)}, u32[]{:S(2)}) collective-permute-start(f32[]{:T(128)} %add.35), channel_id=1, source_target_pairs={{0,2},{1,3},{2,0},{3,1},{4,6},{5,7},{6,4},{7,5},{8,10},{9,11},{10,... | collective-permute-start | bytes 20 | tf_op jit(solution)/shard_map/ppermute | solution.py:11
  253.2 4.2 %collective-permute-start.10 = (f32[]{:T(128)}, f32[]{:T(128)}, u32[]{:S(2)}, u32[]{:S(2)}) collective-permute-start(f32[]{:T(128)} %add.36), channel_id=1, source_target_pairs={{0,4},{1,5},{2,6},{3,7},{4,0},{5,1},{6,2},{7,3},{8,12},{9,13},{10,... | collective-permute-start | bytes 20 | tf_op jit(solution)/shard_map/ppermute | solution.py:11
  258.0 5.1 %collective-permute-start.11 = (f32[]{:T(128)}, f32[]{:T(128)}, u32[]{:S(2)}, u32[]{:S(2)}) collective-permute-start(f32[]{:T(128)} %add.37), channel_id=1, source_target_pairs={{0,8},{1,9},{2,10},{3,11},{4,12},{5,13},{6,14},{7,15},{8,0},{9,1},... | collective-permute-start | bytes 20 | tf_op jit(solution)/shard_map/ppermute | solution.py:11
  264.8 15.1 %all-to-all-start.1 = ((bf16[32,2,1024]{2,1,0:T(2,128)(2,1)}), bf16[32,2,1024]{2,1,0:T(2,128)(2,1)S(1)}, u32[]{:S(2)}, u32[]{:S(2)}) async-start(bf16[32,2,1024]{2,1,0:T(2,128)(2,1)} %reshape.61), calls=%async_computation.1 | async-start | bytes 262144 | tf_op jit(solution)/shard_map/all_to_all | solution.py:67
  268.6 51.3 %all-gather.2.cloned.1.call-start = ((), (), s32[]{:S(2)}) async-start(), calls=%async_computation.2 | async-start | bytes 2228224 | tf_op jit(solution)/shard_map/all_gather | solution.py:70
  281.0 2.0 copy-start.1
Sparse Core Ops, SparseCore 0:
  281.9 38.0 all-gather.1
where the time goes:
time: 331 us; the launch traced here: 330 us
  waiting for transfers between devices  229 us (69%)
  starting transfers between devices  34.3 us (10%)
  blocking collectives  27.6 us (8%)
  between operations  18.1 us (5%)
  local copies, waits for them, and re-layouts  9.09 us (3%)
  other arithmetic  7.65 us (2%)
  matrix products  4.51 us (1%)
    ppermute x12, waiting for transfers between devices, swapped(): lax.ppermute(x, axis, [(i, i ^ 1 << distance) for i in range(lax.axis_siz...  182 us
    all_gather x1, waiting for transfers between devices, body(): lax.all_gather(placed.reshape(shard_rows, groups * width), 'rep', axis=1,...  35.5 us
    ppermute x12, starting transfers between devices, swapped(): lax.ppermute(x, axis, [(i, i ^ 1 << distance) for i in range(lax.axis_siz...  30.4 us
    all_to_all x1, blocking collectives, body(): lax.all_to_all(ordered.reshape(shard_rows, groups * width), 'fsdp', split...  27.6 us
    all_to_all x1, waiting for transfers between devices, body(): lax.all_to_all(scaled, 'fsdp', split_axis=0, concat_axis=1, tiled=True)  11.2 us
  transfers between devices with their start and end apart: 14, of which 14 were waited for; matrix products, arithmetic and copies ran while one was open for 1% of the time, Pallas kernels for 0%

commit v1 on v0

v1 whole, which is shorter than its diff:
```python
import jax
import jax.numpy as jnp
from jax import lax
from jax.experimental import pallas as pl
from jax.experimental.pallas import tpu as pltpu
from jax.sharding import PartitionSpec as P

BETA = 0.9
EPSILON = 1e-06
MESH = pl.DeviceIdType.MESH
F32 = jnp.float32
BF16 = jnp.bfloat16
NT = (((1,), (1,)), ((), ()))


def kernel(
    grad_in, table, lf_in, rf_in, lr_in, rr_in,
    upd_out, left_out, right_out,
    raw, other, gbuf, abuf, bbuf, lbuf, pbuf, home, ubuf, lf, rf, wide, scy, sct, sch,
    lsem, ssem, rsem, hsem, zsem, hsend, zsend,
):
    r = lax.axis_index("rep")
    f = lax.axis_index("fsdp")
    z, y = f // 4, f % 4
    g, p = z // 4, z % 4
    x, yl, c = r // 4, (r // 2) % 2, r % 2
    yn, yp, yo = (y + 1) % 4, (y + 3) % 4, (y + 2) % 4
    zm = 7 - z

    def fdev(zz, yy):
        return {"fsdp": zz * 4 + yy}

    up, down, north, south, mirror = fdev((z + 1) % 8, y), fdev((z + 7) % 8, y), fdev(z, yn), fdev(z, yp), fdev(zm, y)
    r_sib, r_ylo = r + 1 - 2 * c, r + 2 - 4 * yl
    r_xp, r_xm = ((x + 1) % 4) * 4 + r % 4, ((x + 3) % 4) * 4 + r % 4
    sib, ylo, xp, xm = {"rep": r_sib}, {"rep": r_ylo}, {"rep": r_xp}, {"rep": r_xm}

    def load(src, dst, k):
        copy = pltpu.make_async_copy(src, dst, lsem.at[k])
        copy.start()
        return copy

    ld_g = load(grad_in, raw, 0)
    ld_a = load(lr_in.at[0], abuf.at[p], 1)
    ld_b = load(rr_in.at[0], bbuf.at[y], 2)
    ld_l = load(lf_in.at[0], lf, 3)
    ld_r = load(rf_in.at[0], rf, 4)

    barrier = pltpu.get_barrier_semaphore()
    near = (up, down, north, south, mirror, sib, ylo, xp, xm)
    for dev in near:
        pl.semaphore_signal(barrier, inc=1, device_id=dev, device_id_type=MESH)

    pending = []
    counter = [0, 0]

    def new_recv():
        counter[1] += 1
        return rsem.at[counter[1] - 1]

    def send(src, dst, dev, arrival, pred=None):
        copy = pltpu.make_async_remote_copy(
            src_ref=src, dst_ref=dst, send_sem=ssem.at[counter[0]], recv_sem=arrival,
            device_id=dev, device_id_type=MESH,
        )
        counter[0] += 1
        if pred is None:
            copy.start()
        else:
            pl.when(pred)(copy.start)
        pending.append((copy, pred))

    def arrive(dst, arrival, pred=None):
        copy = pltpu.make_async_remote_copy(
            src_ref=dst, dst_ref=dst, send_sem=ssem.at[0], recv_sem=arrival,
            device_id=north, device_id_type=MESH,
        )
        if pred is None:
            copy.wait_recv()
        else:
            pl.when(pred)(copy.wait_recv)

    class Line:
        def __init__(self, slot):
            self.slot = slot
            self.plus = [None] + [new_recv() for _ in range(3)]
            self.minus = [None] + [new_recv() for _ in range(3)]

        def hop(self, d):
            if d >= 2:
                arrive(self.slot(jnp.maximum(z - d + 1, 0)), self.plus[d - 1], p >= d - 1)
            if d <= 3:
                src = self.slot(jnp.maximum(z - d + 1, 0))
                send(src, src, up, self.plus[d], (p >= d - 1) & (p <= 2))
            if d >= 2:
                arrive(self.slot(jnp.minimum(z + d - 1, 7)), self.minus[d - 1], p <= 4 - d)
            if d <= 3:
                src = self.slot(jnp.minimum(z + d - 1, 7))
                send(src, src, down, self.minus[d], (p <= 4 - d) & (p >= 1))

    class Ring:
        def __init__(self, slot, first, second):
            self.slot, self.first, self.second = slot, first, second
            self.sems = [new_recv() for _ in range(4)]

        def start(self):
            for dev, sem in ((north, self.sems[0]), (south, self.sems[1])):
                send(self.slot(y), self.slot(y), dev, sem)

        def forward(self):
            arrive(self.slot(yp), self.sems[0])
            if self.first is not None:
                send(self.first(yp), self.first(yp), north, self.sems[2])
            arrive(self.slot(yn), self.sems[1])
            if self.second is not None:
                send(self.second(yn), self.second(yn), south, self.sems[3])

        def finish(self):
            if self.first is not None:
                arrive(self.first(yo), self.sems[2])
            if self.second is not None:
                arrive(self.second(yo), self.sems[3])

    ld_g.wait()
    swap = table[r, 0] != 0
    first_is_mine = jnp.where(swap, g == 1, g == 0)
    lo, hi = raw[:, 0:1024], raw[:, 1024:2048]
    mine = jnp.where(first_is_mine, lo, hi)
    theirs = jnp.where(first_is_mine, hi, lo)
    for h in range(2):
        gbuf[h, z, y] = mine[:, 512 * h:512 * h + 512]
        other[h] = theirs[:, 512 * h:512 * h + 512]

    pl.semaphore_wait(barrier, len(near))

    esem = [new_recv() for _ in range(2)]
    for h in range(2):
        send(other.at[h], gbuf.at[h, z, y], mirror, esem[h])

    def slot0(zz):
        return lambda yy: gbuf.at[0, zz, yy]

    ring_a = Ring(slot0(z), slot0(z), None)
    ring_b = Ring(slot0(zm), None, slot0(zm))
    line_a = Line(lambda zz: gbuf.at[1, zz, y])
    line_b = Line(lambda zz: gbuf.at[1, 7 - zz, y])
    slab_a = Line(lambda zz: gbuf.at[0, zz])
    slab_b = Line(lambda zz: gbuf.at[0, 7 - zz])
    ring_s = Ring(
        lambda yy: gbuf.at[1, :, yy],
        lambda yy: gbuf.at[1, pl.ds(0, 4), yy],
        lambda yy: gbuf.at[1, pl.ds(4, 4), yy],
    )
    line_r = Line(lambda zz: abuf.at[zz % 4])
    ring_r = Ring(
        lambda yy: bbuf.at[yy],
        lambda yy: bbuf.at[yy, pl.ds(0, 32)],
        lambda yy: bbuf.at[yy, pl.ds(32, 32)],
    )

    ring_a.start()
    line_a.hop(1)
    arrive(gbuf.at[0, zm, y], esem[0])
    ring_b.start()
    arrive(gbuf.at[1, zm, y], esem[1])
    line_b.hop(1)
    ring_a.forward()
    line_a.hop(2)
    ring_b.forward()
    line_b.hop(2)
    ring_a.finish()
    slab_a.hop(1)
    ring_b.finish()
    slab_b.hop(1)
    line_a.hop(3)
    line_b.hop(3)
    line_a.hop(4)
    line_b.hop(4)
    ring_s.start()
    ld_a.wait()
    line_r.hop(1)
    ld_b.wait()
    ring_r.start()
    slab_a.hop(2)
    slab_b.hop(2)
    ring_s.forward()
    slab_a.hop(3)
    slab_b.hop(3)
    line_r.hop(2)
    ring_r.forward()
    line_r.hop(3)
    line_r.hop(4)
    slab_a.hop(4)
    slab_b.hop(4)

    def left_half(h):
        def step(t, _):
            cols = pl.ds(pl.multiple_of(t * 256, 256), 256)
            g_cols = gbuf[h, :, :, :, cols].reshape(1024, 256)
            prod = jnp.dot(abuf[...].reshape(256, 1024), g_cols, preferred_element_type=F32)
            lbuf[:, pl.ds(pl.multiple_of(512 * h + t * 256, 256), 256)] = prod.astype(BF16)
            return 0
        lax.fori_loop(0, 2, step, 0)

    left_half(0)
    ring_s.finish()
    left_half(1)
    ring_r.finish()
    prod = lax.dot_general(lbuf[...], bbuf[...].reshape(256, 1024), NT, preferred_element_type=F32)
    pbuf[...] = prod.astype(BF16).reshape(4, 2, 32, 256)

    homes = [(2 * q + y // 2, 2 * (y % 2) + j, q, j) for q in range(4) for j in range(2)]
    me = 4 * g + p
    mycols = pl.ds(pl.multiple_of(256 * p, 256), 256)

    def to_homes(pick, place, arrivals, sends):
        for k, (hz, hy, q, j) in enumerate(homes):
            itself = (hz == z) & (hy == y)
            away = pltpu.make_async_remote_copy(
                src_ref=pick(q, j), dst_ref=place, send_sem=sends.at[k], recv_sem=arrivals.at[me],
                device_id=fdev(hz, hy), device_id_type=MESH,
            )
            here = pltpu.make_async_copy(pick(q, j), place, arrivals.at[me])
            pl.when(itself)(here.start)
            pl.when(jnp.logical_not(itself))(away.start)
            pending.append((away, jnp.logical_not(itself)))

    to_homes(lambda q, j: pbuf.at[q, j], home.at[g, :, mycols], hsem, hsend)

    squares = jnp.sum(jnp.sum(prod * prod, axis=0, keepdims=True), axis=1, keepdims=True)
    scy[y] = jnp.broadcast_to(squares, (8, 128))
    ysem = [new_recv() for _ in range(3)]
    for d in range(1, 4):
        send(scy.at[y], scy.at[y], fdev(z, (y + d) % 4), ysem[d - 1])

    def add_squares(t, total):
        part = gbuf[t // 8, t % 8].reshape(128, 512).astype(F32)
        return total + jnp.sum(part * part, axis=0, keepdims=True)

    grad_squares = lax.fori_loop(0, 16, add_squares, jnp.zeros((1, 512), F32))
    sct[1] = jnp.broadcast_to(jnp.sum(grad_squares, axis=1, keepdims=True), (8, 128))
    for d in range(1, 4):
        arrive(scy.at[(y + 4 - d) % 4], ysem[d - 1])
    sct[0] = scy[0] + scy[1] + scy[2] + scy[3]
    to_homes(lambda q, j: sct, sch.at[me], zsem, zsend)

    ld_l.wait()
    own = [gbuf[h, 2 * p + y // 2, pl.ds(2 * (y % 2), 2)].reshape(64, 512) for h in range(2)]
    for t in range(4):
        stat = jnp.zeros((64, 256), F32)
        for h in range(2):
            rows = gbuf[h, pl.ds(2 * t, 2)].reshape(256, 512)
            stat = stat + lax.dot_general(own[h], rows, NT, preferred_element_type=F32)
        cols = slice(256 * t, 256 * t + 256)
        lf[:, cols] = BETA * lf[:, cols] + (1.0 - BETA) / 1024 * stat
    st_l = pltpu.make_async_copy(lf, left_out.at[0], lsem.at[3])
    st_l.start()

    for k in range(8):
        arrive(home.at[k // 4, :, pl.ds(256 * (k % 4), 256)], hsem.at[k])
    for k in range(8):
        arrive(sch.at[k], zsem.at[k])
    done = []
    for q in range(2):
        total = sch[4 * q, 0] + sch[4 * q + 1, 0] + sch[4 * q + 2, 0] + sch[4 * q + 3, 0]
        ratio = jnp.sqrt(sch[4 * q, 1]) / jnp.sqrt(total + EPSILON)
        done.append((home[q].astype(F32) * ratio[0:1, 0:1]).astype(BF16))

    def slot(rr):
        return ubuf.at[:, pl.ds(pl.multiple_of(rr * 2048, 2048), 2048)]

    def part(rr, k):
        return ubuf.at[pl.ds(16 * k, 16), pl.ds(pl.multiple_of(rr * 2048, 2048), 2048)]

    ubuf[:, pl.ds(pl.multiple_of(r * 2048, 2048), 1024)] = jnp.where(swap, done[1], done[0])
    ubuf[:, pl.ds(pl.multiple_of(r * 2048 + 1024, 1024), 1024)] = jnp.where(swap, done[0], done[1])

    sib_waits = []

    def share(ref_of, rr):
        sem = new_recv()
        send(ref_of(rr), ref_of(rr), sib, sem)
        sib_waits.append((ref_of(rr + 1 - 2 * c), sem))

    y_sem = new_recv()
    xps, xms, xpf, xmf = ([new_recv() for _ in range(2)] for _ in range(4))
    send(slot(r), slot(r), ylo, y_sem)
    send(slot(r), slot(r), xp, xps[0])
    send(slot(r), slot(r), xm, xms[0])
    share(slot, r)

    def rep_of(q, dx):
        return ((x + dx + 4) % 4) * 4 + (yl + q - 2 * yl * q) * 2 + c

    arrive(slot(r_ylo), y_sem)
    send(slot(r_ylo), slot(r_ylo), xp, xps[1])
    send(slot(r_ylo), slot(r_ylo), xm, xms[1])
    share(slot, r_ylo)
    for q in range(2):
        before, after = rep_of(q, -1), rep_of(q, 1)
        arrive(slot(before), xps[q])
        send(part(before, 0), part(before, 0), xp, xpf[q])
        share(slot, before)
        arrive(slot(after), xms[q])
        send(part(after, 1), part(after, 1), xm, xmf[q])
        share(slot, after)

    ld_r.wait()
    lanes = pl.ds(pl.multiple_of(128 * (2 * (p % 2) + y // 2), 128), 128)
    turned = gbuf[p // 2, :, :, :, lanes].reshape(1024, 128).T
    for t in range(4):
        g_cols = gbuf[t // 2, :, :, :, 256 * (t % 2):256 * (t % 2) + 256].reshape(1024, 256)
        wide[:, 256 * t:256 * t + 256] = jnp.dot(turned, g_cols, preferred_element_type=F32)
    rf[...] = BETA * rf[...] + (1.0 - BETA) / 1024 * wide[pl.ds(pl.multiple_of(64 * (y % 2), 64), 64), :]
    st_r = pltpu.make_async_copy(rf, right_out.at[0], lsem.at[4])
    st_r.start()

    for q in range(2):
        across = rep_of(q, 2)
        arrive(part(across, 0), xpf[q])
        share(lambda rr: part(rr, 0), across)
        arrive(part(across, 1), xmf[q])
        share(lambda rr: part(rr, 1), across)
    for ref, sem in sib_waits:
        arrive(ref, sem)
    st_u = pltpu.make_async_copy(ubuf, upd_out, lsem.at[0])
    st_u.start()
    for copy, pred in pending:
        if pred is None:
            copy.wait_send()
        else:
            pl.when(pred)(copy.wait_send)
    st_l.wait()
    st_r.wait()
    st_u.wait()


def body(gradient, owner_table, left_factor, right_factor, left_root, right_root):
    vmem = pltpu.VMEM
    anywhere = pl.BlockSpec(memory_space=pl.ANY)
    return pl.pallas_call(
        kernel,
        out_shape=(
            jax.ShapeDtypeStruct((32, 32768), BF16),
            jax.ShapeDtypeStruct((1, 64, 1024), F32),
            jax.ShapeDtypeStruct((1, 64, 1024), F32),
        ),
        in_specs=[anywhere, pl.BlockSpec(memory_space=pltpu.SMEM)] + [anywhere] * 4,
        out_specs=(anywhere,) * 3,
        scratch_shapes=[
            vmem((32, 2048), BF16),
            vmem((2, 32, 512), BF16),
            vmem((2, 8, 4, 32, 512), BF16),
            vmem((4, 64, 1024), BF16),
            vmem((4, 64, 1024), BF16),
            vmem((256, 1024), BF16),
            vmem((4, 2, 32, 256), BF16),
            vmem((2, 32, 1024), BF16),
            vmem((32, 32768), BF16),
            vmem((64, 1024), F32),
            vmem((64, 1024), F32),
            vmem((128, 1024), F32),
            vmem((4, 8, 128), F32),
            vmem((2, 8, 128), F32),
            vmem((8, 2, 8, 128), F32),
            pltpu.SemaphoreType.DMA((5,)),
            pltpu.SemaphoreType.DMA((80,)),
            pltpu.SemaphoreType.DMA((80,)),
            pltpu.SemaphoreType.DMA((8,)),
            pltpu.SemaphoreType.DMA((8,)),
            pltpu.SemaphoreType.DMA((8,)),
            pltpu.SemaphoreType.DMA((8,)),
        ],
        compiler_params=pltpu.CompilerParams(
            collective_id=0, has_side_effects=True, vmem_limit_bytes=40 * 1024 * 1024
        ),
    )(gradient, owner_table, left_factor, right_factor, left_root, right_root)


def solution(mesh):
    placed = (
        P("fsdp", "rep"),
        P(),
        P("rep", "fsdp", None),
        P("rep", "fsdp", None),
        P("rep", "fsdp", None),
        P("rep", "fsdp", None),
    )
    return jax.shard_map(
        body,
        mesh=mesh,
        in_specs=placed,
        out_specs=(P("fsdp", None), P("rep", "fsdp", None), P("rep", "fsdp", None)),
        check_vma=False,
    )
```

time: 331 us -> 98 us (0.30)
  waiting for transfers between devices: 229 us -> 0 us
  Pallas kernels: 0 us -> 89 us
  starting transfers between devices: 34.3 us -> 0 us
  blocking collectives: 27.6 us -> 0 us
  between operations: 18.1 us -> 0.64 us
  other arithmetic: 7.65 us -> 0 us
  matrix products: 4.51 us -> 0 us
    ppermute x12 -> x0, waiting for transfers between devices: 182 us -> none  [swapped(): lax.ppermute(x, axis, [(i, i ^ 1 << distance) for i in range(lax.axis_siz...]
    pallas_call x0 -> x1, Pallas kernels: none -> 89 us  [body(): pl.pallas_call(kernel, out_shape=(jax.ShapeDtypeStruct((32, 32768), BF16)...]
    all_gather x1 -> x0, waiting for transfers between devices: 35.5 us -> none  [body(): lax.all_gather(placed.reshape(shard_rows, groups * width), 'rep', axis=1,...]
    ppermute x12 -> x0, starting transfers between devices: 30.4 us -> none  [swapped(): lax.ppermute(x, axis, [(i, i ^ 1 << distance) for i in range(lax.axis_siz...]
    all_to_all x1 -> x0, blocking collectives: 27.6 us -> none  [body(): lax.all_to_all(ordered.reshape(shard_rows, groups * width), 'fsdp', split...]
    all_to_all x1 -> x0, waiting for transfers between devices: 11.2 us -> none  [body(): lax.all_to_all(scaled, 'fsdp', split_axis=0, concat_axis=1, tiled=True)]
    dot_general x4 -> x0, matrix products: 4.51 us -> none  [the longest x1 1.45 us: body(): lax.dot_general(own_rows, block, (((1,), (1,)), ((), ())), preferred_elem...]
    select_n x10 -> x0, other arithmetic: 4.35 us -> none  [the longest x8 4.26 us: paired(): first = jnp.where(lower, mine, other)]
  transfers between devices with their start and end apart: 14 -> 0, of which waited for: 14 -> 0; matrix products, arithmetic and copies ran while one was open for 1% -> 0% of each run, Pallas kernels for 0% -> 0%
where the time goes in v1:
time: 98 us; the launch traced here: 97.7 us
  Pallas kernels  89 us (91%)
  local copies, waits for them, and re-layouts  8.09 us (8%)
    pallas_call x1, Pallas kernels, body(): pl.pallas_call(kernel, out_shape=(jax.ShapeDtypeStruct((32, 32768), BF16)...  89 us
    unnamed x14, local copies, waits for them, and re-layouts  8.09 us

profile of v1, /device:TPU:1, one launch (start us, length us, event | category | flops | bytes accessed | tf_op | source)
XLA Modules:
  0.0 97.7 jit_solution(14582912425503342525)
XLA Ops:
  0.6 0.8 copy.9.table
  1.4 0.0 copy-start
  1.4 0.9 copy-done
  2.3 0.0 copy-start.1
  2.3 0.9 copy-done.1
  3.3 0.0 copy-start.2
  3.3 0.9 copy-done.2
  4.2 0.0 copy-start.3
  4.2 0.9 copy-done.3
  5.1 0.0 copy-start.4
  5.1 0.9 copy-done.4
  6.0 89.0 %shard_map.85 = (bf16[32,32768]{1,0:T(8,128)(2,1)S(1)}, f32[1,64,1024]{2,1,0:T(8,128)S(1)}, f32[1,64,1024]{2,1,0:T(8,128)S(1)}) custom-call(bf16[32,2048]{1,0:T(8,128)(2,1)S(1)} %copy-done.2, s32[16,2]{1,0:T(8,128)S(1)} %copy.9.table, f32[1,64,1024]{2,1,0:T(8,128)S(1)} %copy-done, f32[1,64,1024]{2,1,0:T(8,128)S(1)} %copy-done.1, ...), custom_call_target="tpu_custom_call" | custom-call | tf_op jit(solution)/shard_map/pallas_call | solution.py:341
  95.0 1.3 %copy.13 = bf16[32,32768]{1,0:T(8,128)(2,1)} copy(bf16[32,32768]{1,0:T(8,128)(2,1)S(1)} %get-tuple-element.6) | data formatting | bytes 4194304
  96.3 0.7 copy.14
  97.0 0.7 copy.15
Async XLA Ops:
  1.4 0.9 copy-start
  2.3 0.9 copy-start.1
  3.3 0.9 copy-start.2
  4.2 0.9 copy-start.3
  5.1 0.9 copy-start.4

commit v2 on v1

v2 whole, which is shorter than its diff:
```python
import jax
import jax.numpy as jnp
from jax import lax
from jax.experimental import pallas as pl
from jax.experimental.pallas import tpu as pltpu
from jax.sharding import PartitionSpec as P

BETA = 0.9
EPSILON = 1e-06
MESH = pl.DeviceIdType.MESH
F32 = jnp.float32
BF16 = jnp.bfloat16
NT = (((1,), (1,)), ((), ()))


def kernel(
    grad_in, table_in, lf_in, rf_in, lr_in, rr_in,
    upd, left_out, right_out,
    table, raw, strips, gbuf, abuf, bbuf, lbuf, pbuf, home, own, lf, rf, wide, sums,
    lsem, ssem, rsem, hsem, zsem, hsend,
):
    r = lax.axis_index("rep")
    f = lax.axis_index("fsdp")
    z, y = f // 4, f % 4
    g, p = z // 4, z % 4
    x, yl, c = r // 4, (r // 2) % 2, r % 2
    yn, yp, yo = (y + 1) % 4, (y + 3) % 4, (y + 2) % 4

    def fdev(zz, yy):
        return {"fsdp": zz * 4 + yy}

    up, down, north, south = fdev((z + 1) % 8, y), fdev((z + 7) % 8, y), fdev(z, yn), fdev(z, yp)
    r_sib, r_ylo = r + 1 - 2 * c, r + 2 - 4 * yl
    sib, ylo = {"rep": r_sib}, {"rep": r_ylo}
    xp, xm, xo = ({"rep": ((x + d) % 4) * 4 + r % 4} for d in (1, 3, 2))

    barrier = pltpu.get_barrier_semaphore()
    near = [fdev((z + d) % 8, y) for d in (1, 7, 2, 6, 3, 5, 4)] + [north, south, sib, ylo, xp, xm, xo]
    for dev in near:
        pl.semaphore_signal(barrier, inc=1, device_id=dev, device_id_type=MESH)

    def load(src, dst, k):
        copy = pltpu.make_async_copy(src, dst, lsem.at[k])
        copy.start()
        return copy

    ld_g = load(grad_in, raw, 0)
    ld_t = load(table_in, table, 5)
    ld_a = load(lr_in.at[0], abuf.at[p], 1)
    ld_b = load(rr_in.at[0], bbuf.at[y], 2)
    ld_l = load(lf_in.at[0], lf, 3)
    ld_r = load(rf_in.at[0], rf, 4)

    pending = []
    counter = [0, 0]

    def new_recv():
        counter[1] += 1
        return rsem.at[counter[1] - 1]

    def send(src, dst, dev, arrival, pred=None):
        copy = pltpu.make_async_remote_copy(
            src_ref=src, dst_ref=dst, send_sem=ssem.at[counter[0]], recv_sem=arrival,
            device_id=dev, device_id_type=MESH,
        )
        counter[0] += 1
        if pred is None:
            copy.start()
        else:
            pl.when(pred)(copy.start)
        pending.append((copy, pred))

    def arrive(dst, arrival, pred=None):
        copy = pltpu.make_async_remote_copy(
            src_ref=dst, dst_ref=dst, send_sem=ssem.at[0], recv_sem=arrival,
            device_id=north, device_id_type=MESH,
        )
        if pred is None:
            copy.wait_recv()
        else:
            pl.when(pred)(copy.wait_recv)

    class Line:
        def __init__(self, slot):
            self.slot = slot
            self.plus = [None] + [new_recv() for _ in range(3)]
            self.minus = [None] + [new_recv() for _ in range(3)]

        def hop(self, d):
            if d >= 2:
                arrive(self.slot(jnp.maximum(z - d + 1, 0)), self.plus[d - 1], p >= d - 1)
            if d <= 3:
                src = self.slot(jnp.maximum(z - d + 1, 0))
                send(src, src, up, self.plus[d], (p >= d - 1) & (p <= 2))
            if d >= 2:
                arrive(self.slot(jnp.minimum(z + d - 1, 7)), self.minus[d - 1], p <= 4 - d)
            if d <= 3:
                src = self.slot(jnp.minimum(z + d - 1, 7))
                send(src, src, down, self.minus[d], (p <= 4 - d) & (p >= 1))

    class Ring:
        def __init__(self, slot, first, second):
            self.slot, self.first, self.second = slot, first, second
            self.sems = [new_recv() for _ in range(4)]

        def start(self):
            for dev, sem in ((north, self.sems[0]), (south, self.sems[1])):
                send(self.slot(y), self.slot(y), dev, sem)

        def forward(self):
            arrive(self.slot(yp), self.sems[0])
            send(self.first(yp), self.first(yp), north, self.sems[2])
            arrive(self.slot(yn), self.sems[1])
            send(self.second(yn), self.second(yn), south, self.sems[3])

        def finish(self):
            arrive(self.first(yo), self.sems[2])
            arrive(self.second(yo), self.sems[3])

    ld_g.wait()
    ld_t.wait()
    swap = table[0, r] != 0
    lo, hi = raw[:, 0:1024], raw[:, 1024:2048]
    for q in range(2):
        block = jnp.where(swap, hi, lo) if q == 0 else jnp.where(swap, lo, hi)
        for s in range(4):
            strips[4 * q + s] = block[:, 256 * s:256 * s + 256]
    gbuf[p, z, y] = strips[z]

    pl.semaphore_wait(barrier, len(near))

    asem = [new_recv() for _ in range(8)]
    for d in (4, 3, 5, 2, 6, 1, 7):
        zz = (z + d) % 8
        send(strips.at[zz], gbuf.at[zz % 4, z, y], fdev(zz, y), asem[d])

    def ring_of(s):
        return Ring(
            lambda yy: gbuf.at[s, :, yy],
            lambda yy: gbuf.at[s, pl.ds(0, 4), yy],
            lambda yy: gbuf.at[s, pl.ds(4, 4), yy],
        )

    ring_p = ring_of(p)
    others = [(p + d) % 4 for d in range(1, 4)]
    rings = [ring_of(s) for s in others]
    line_r = Line(lambda zz: abuf.at[zz % 4])
    line_g = Line(lambda zz: gbuf.at[zz % 4, :, y])
    ring_r = Ring(
        lambda yy: bbuf.at[yy],
        lambda yy: bbuf.at[yy, pl.ds(0, 32)],
        lambda yy: bbuf.at[yy, pl.ds(32, 32)],
    )

    ld_a.wait()
    line_r.hop(1)
    ld_b.wait()
    ring_r.start()
    for d in (1, 7, 2, 6, 3, 5, 4):
        arrive(gbuf.at[p, (z + 8 - d) % 8, y], asem[d])
    ring_p.start()
    line_g.hop(1)
    line_r.hop(2)
    ring_r.forward()
    line_r.hop(3)
    line_g.hop(2)
    ring_p.forward()
    line_r.hop(4)
    line_g.hop(3)
    ring_p.finish()

    lbuf[p] = jnp.dot(
        abuf[...].reshape(256, 1024), gbuf[p].reshape(1024, 256), preferred_element_type=F32
    ).astype(BF16)
    psem = [new_recv() for _ in range(4)]
    for d in (1, 3, 2):
        send(lbuf.at[p], lbuf.at[p], fdev(4 * g + (p + d) % 4, y), psem[d])
    line_g.hop(4)
    for ring in rings:
        ring.start()

    def add_squares(t, total):
        part = gbuf[p, t].reshape(128, 256).astype(F32)
        return total + jnp.sum(part * part, axis=0, keepdims=True)

    grad_squares = lax.fori_loop(0, 8, add_squares, jnp.zeros((1, 256), F32))
    grad_squares = 0.25 * jnp.sum(grad_squares, axis=1, keepdims=True)

    scale = (1.0 - BETA) / 1024
    my_z, my_y = 2 * p + y // 2, 2 * (y % 2)
    lanes = pl.ds(pl.multiple_of(128 * (y // 2), 128), 128)

    def statistics(s):
        mine = gbuf[s, my_z, pl.ds(my_y, 2)].reshape(64, 256)
        for t in range(4):
            rows = gbuf[s, pl.ds(2 * t, 2)].reshape(256, 256)
            lf[:, 256 * t:256 * t + 256] += scale * lax.dot_general(mine, rows, NT, preferred_element_type=F32)
        turned = gbuf[p, :, :, :, lanes].reshape(1024, 128).T
        wide[...] = jnp.dot(turned, gbuf[s].reshape(1024, 256), preferred_element_type=F32)
        cols = pl.ds(pl.multiple_of(256 * s, 256), 256)
        rf[:, cols] = BETA * rf[:, cols] + scale * wide[pl.ds(pl.multiple_of(64 * (y % 2), 64), 64), :]

    ld_l.wait()
    ld_r.wait()
    lf[...] = BETA * lf[...]
    statistics(p)
    ring_r.finish()

    def tile_part(s):
        cols = pl.ds(pl.multiple_of(256 * s, 256), 256)
        return lax.dot_general(lbuf[s], bbuf[:, :, cols].reshape(256, 256), NT, preferred_element_type=F32)

    prod = tile_part(p)
    for d in (1, 3, 2):
        s = (p + 4 - d) % 4
        arrive(lbuf.at[s], psem[d])
        prod = prod + tile_part(s)
    pbuf[...] = prod.astype(BF16).reshape(4, 2, 32, 256)

    mycols = pl.ds(pl.multiple_of(256 * p, 256), 256)
    for q in range(4):
        for j in range(2):
            k, hz, hy = 2 * q + j, 2 * q + y // 2, 2 * (y % 2) + j
            itself = (hz == z) & (hy == y)
            src, place, arrival = pbuf.at[q, j], home.at[g, :, mycols], hsem.at[4 * g + p]
            away = pltpu.make_async_remote_copy(
                src_ref=src, dst_ref=place, send_sem=hsend.at[k], recv_sem=arrival,
                device_id=fdev(hz, hy), device_id_type=MESH,
            )
            here = pltpu.make_async_copy(src, place, arrival)
            pl.when(itself)(here.start)
            pl.when(jnp.logical_not(itself))(away.start)
            pending.append((away, jnp.logical_not(itself)))
    squares = jnp.sum(jnp.sum(prod * prod, axis=0, keepdims=True), axis=1, keepdims=True)
    row = lax.broadcasted_iota(jnp.int32, (8, 128), 0)
    sums[f] = jnp.where(row < 4, squares, grad_squares)

    def tell(d, _):
        pltpu.make_async_remote_copy(
            src_ref=sums.at[f], dst_ref=sums.at[f], send_sem=zsem.at[0], recv_sem=zsem.at[1],
            device_id={"fsdp": (f + d) % 32}, device_id_type=MESH,
        ).start()
        return 0

    lax.fori_loop(1, 32, tell, 0)
    rings[0].forward()

    for k in range(8):
        arrive(home.at[k // 4, :, pl.ds(256 * (k % 4), 256)], hsem.at[k])
    everyone = pltpu.make_async_remote_copy(
        src_ref=sums.at[pl.ds(0, 31)], dst_ref=sums.at[pl.ds(0, 31)], send_sem=zsem.at[0], recv_sem=zsem.at[1],
        device_id=north, device_id_type=MESH,
    )
    everyone.wait_recv()
    done = []
    for q in range(2):
        total = jnp.sum(sums[16 * q:16 * q + 16], axis=0)
        ratio = jnp.sqrt(total[4:5, 0:1]) / jnp.sqrt(total[0:1, 0:1] + EPSILON)
        done.append((home[q].astype(F32) * ratio).astype(BF16))
    own[:, 0:1024] = jnp.where(swap, done[1], done[0])
    own[:, 1024:2048] = jnp.where(swap, done[0], done[1])

    def slot(rr):
        return upd.at[:, pl.ds(pl.multiple_of(rr * 2048, 2048), 2048)]

    sib_waits = []

    def share(rr, src=None):
        sem = new_recv()
        send(slot(rr) if src is None else src, slot(rr), sib, sem)
        sib_waits.append((slot(rr + 1 - 2 * c), sem))

    def rep_of(q, dx):
        return ((x + dx + 4) % 4) * 4 + (yl + q - 2 * yl * q) * 2 + c

    y_sem = new_recv()
    xsem = [[new_recv() for _ in range(4)] for _ in range(2)]
    send(own, slot(r), ylo, y_sem)
    for d in (1, 3, 2):
        send(own, slot(r), {"rep": rep_of(0, d)}, xsem[0][d])
    share(r, own)
    keep = pltpu.make_async_copy(own, slot(r), lsem.at[0])
    keep.start()
    rings[1].forward()
    arrive(slot(r_ylo), y_sem)
    for d in (1, 3, 2):
        send(slot(r_ylo), slot(r_ylo), {"rep": rep_of(0, d)}, xsem[1][d])
    share(r_ylo)
    rings[2].forward()
    for q in range(2):
        for d in (1, 3, 2):
            arrive(slot(rep_of(q, -d)), xsem[q][d])
            share(rep_of(q, -d))
    for ring, s in zip(rings, others):
        ring.finish()
        statistics(s)
    st_l = pltpu.make_async_copy(lf, left_out.at[0], lsem.at[3])
    st_l.start()
    st_r = pltpu.make_async_copy(rf, right_out.at[0], lsem.at[4])
    st_r.start()
    for ref, sem in sib_waits:
        arrive(ref, sem)
    for copy, pred in pending:
        if pred is None:
            copy.wait_send()
        else:
            pl.when(pred)(copy.wait_send)
    everyone.wait_send()
    keep.wait()
    st_l.wait()
    st_r.wait()


def pinned(array):
    return pltpu.with_memory_space_constraint(array, pltpu.HBM)


def body(gradient, owner_table, left_factor, right_factor, left_root, right_root):
    vmem = pltpu.VMEM
    anywhere = pl.BlockSpec(memory_space=pl.ANY)
    hbm = pl.BlockSpec(memory_space=pltpu.HBM)
    return pl.pallas_call(
        kernel,
        out_shape=(
            vmem((32, 32768), BF16),
            vmem((1, 64, 1024), F32),
            vmem((1, 64, 1024), F32),
        ),
        in_specs=[hbm] * 6,
        out_specs=(anywhere,) * 3,
        scratch_shapes=[
            pltpu.SMEM((2, 16), jnp.int32),
            vmem((32, 2048), BF16),
            vmem((8, 32, 256), BF16),
            vmem((4, 8, 4, 32, 256), BF16),
            vmem((4, 64, 1024), BF16),
            vmem((4, 64, 1024), BF16),
            vmem((4, 256, 256), BF16),
            vmem((4, 2, 32, 256), BF16),
            vmem((2, 32, 1024), BF16),
            vmem((32, 2048), BF16),
            vmem((64, 1024), F32),
            vmem((64, 1024), F32),
            vmem((128, 256), F32),
            vmem((32, 8, 128), F32),
            pltpu.SemaphoreType.DMA((6,)),
            pltpu.SemaphoreType.DMA((80,)),
            pltpu.SemaphoreType.DMA((80,)),
            pltpu.SemaphoreType.DMA((8,)),
            pltpu.SemaphoreType.DMA((2,)),
            pltpu.SemaphoreType.DMA((8,)),
        ],
        compiler_params=pltpu.CompilerParams(
            collective_id=0, has_side_effects=True, vmem_limit_bytes=40 * 1024 * 1024
        ),
    )(
        pinned(gradient), pinned(owner_table.T), pinned(left_factor), pinned(right_factor),
        pinned(left_root), pinned(right_root),
    )


def solution(mesh):
    placed = (
        P("fsdp", "rep"),
        P(),
        P("rep", "fsdp", None),
        P("rep", "fsdp", None),
        P("rep", "fsdp", None),
        P("rep", "fsdp", None),
    )
    return jax.shard_map(
        body,
        mesh=mesh,
        in_specs=placed,
        out_specs=(P("fsdp", None), P("rep", "fsdp", None), P("rep", "fsdp", None)),
        check_vma=False,
    )
```

time: 98 us -> 87.1 us (0.89)
  Pallas kernels: 89 us -> 83.6 us
  local copies, waits for them, and re-layouts: 8.09 us -> 2.73 us
    pallas_call x1, Pallas kernels: 89 us -> 83.6 us  [body(): pl.pallas_call(kernel, out_shape=(vmem((32, 32768), BF16), vmem((1, 64, 1...]
    unnamed x14 -> x3, local copies, waits for them, and re-layouts: 8.09 us -> 2.73 us
where the time goes in v2:
time: 87.1 us; the launch traced here: 86.9 us
  Pallas kernels  83.6 us (96%)
  local copies, waits for them, and re-layouts  2.73 us (3%)
    pallas_call x1, Pallas kernels, body(): pl.pallas_call(kernel, out_shape=(vmem((32, 32768), BF16), vmem((1, 64, 1...  83.6 us
    unnamed x3, local copies, waits for them, and re-layouts  2.73 us

profile of v2, /device:TPU:1, one launch (start us, length us, event | category | flops | bytes accessed | tf_op | source)
XLA Modules:
  0.0 86.9 jit_solution(16127466006285231046)
XLA Ops:
  0.6 83.6 %shard_map.85 = (bf16[32,32768]{1,0:T(8,128)(2,1)S(1)}, f32[1,64,1024]{2,1,0:T(8,128)S(1)}, f32[1,64,1024]{2,1,0:T(8,128)S(1)}) custom-call(bf16[32,2048]{1,0:T(8,128)(2,1)} %grad_in.1, s32[2,16]{1,0:T(2,128)} %bitcast.1, f32[1,64,1024]{2,1,0:T(8,128)} %lf_in.1, f32[1,64,1024]{2,1,0:T(8,128)} %rf_in.1, bf16[1,64,1024]{2,1,0:T(8,128)(2,1)} %lr_in.1, ...), custom_call_target="tpu_custom_call" | custom-call | tf_op jit(solution)/shard_map/pallas_call | solution.py:322
  84.2 1.3 %copy.12 = bf16[32,32768]{1,0:T(8,128)(2,1)} copy(bf16[32,32768]{1,0:T(8,128)(2,1)S(1)} %get-tuple-element.3) | data formatting | bytes 4194304
  85.5 0.7 copy.13
  86.2 0.7 copy.14

commit v3 on v2

--- a/solution.py
+++ b/solution.py
@@ -15,9 +15,9 @@
 
 def kernel(
     grad_in, table_in, lf_in, rf_in, lr_in, rr_in,
-    upd, left_out, right_out,
-    table, raw, strips, gbuf, abuf, bbuf, lbuf, pbuf, home, own, lf, rf, wide, sums,
-    lsem, ssem, rsem, hsem, zsem, hsend,
+    upd, lf_out, rf_out,
+    table, raw, strips, gbuf, abuf, bbuf, lbuf, pbuf, land, wide, sum_y, sum_z, ratio,
+    lsem, ssem, rsem, hsem, tsem, hsend,
 ):
     r = lax.axis_index("rep")
     f = lax.axis_index("fsdp")
@@ -32,10 +32,10 @@
     up, down, north, south = fdev((z + 1) % 8, y), fdev((z + 7) % 8, y), fdev(z, yn), fdev(z, yp)
     r_sib, r_ylo = r + 1 - 2 * c, r + 2 - 4 * yl
     sib, ylo = {"rep": r_sib}, {"rep": r_ylo}
-    xp, xm, xo = ({"rep": ((x + d) % 4) * 4 + r % 4} for d in (1, 3, 2))
 
     barrier = pltpu.get_barrier_semaphore()
-    near = [fdev((z + d) % 8, y) for d in (1, 7, 2, 6, 3, 5, 4)] + [north, south, sib, ylo, xp, xm, xo]
+    near = [fdev((z + d) % 8, y) for d in (1, 7, 2, 6, 3, 5, 4)] + [north, south]
+    near += [{"rep": (r + d) % 16} for d in range(1, 16)]
     for dev in near:
         pl.semaphore_signal(barrier, inc=1, device_id=dev, device_id_type=MESH)
 
@@ -48,6 +48,7 @@
     ld_t = load(table_in, table, 5)
     ld_a = load(lr_in.at[0], abuf.at[p], 1)
     ld_b = load(rr_in.at[0], bbuf.at[y], 2)
+    lf, rf = lf_out.at[0], rf_out.at[0]
     ld_l = load(lf_in.at[0], lf, 3)
     ld_r = load(rf_in.at[0], rf, 4)
 
@@ -134,15 +135,17 @@
         zz = (z + d) % 8
         send(strips.at[zz], gbuf.at[zz % 4, z, y], fdev(zz, y), asem[d])
 
-    def ring_of(s):
+    def ring_of(s, lanes=slice(0, 256)):
         return Ring(
-            lambda yy: gbuf.at[s, :, yy],
-            lambda yy: gbuf.at[s, pl.ds(0, 4), yy],
-            lambda yy: gbuf.at[s, pl.ds(4, 4), yy],
+            lambda yy: gbuf.at[s, :, yy, :, lanes],
+            lambda yy: gbuf.at[s, pl.ds(0, 4), yy, :, lanes],
+            lambda yy: gbuf.at[s, pl.ds(4, 4), yy, :, lanes],
         )
 
-    ring_p = ring_of(p)
-    others = [(p + d) % 4 for d in range(1, 4)]
+    halves = [slice(0, 128), slice(128, 256)]
+    rings_p = [ring_of(p, half) for half in halves]
+    beside = p + 1 - 2 * (p % 2)
+    others = [(p + 2) % 4, 3 - p]
     rings = [ring_of(s) for s in others]
     line_r = Line(lambda zz: abuf.at[zz % 4])
     line_g = Line(lambda zz: gbuf.at[zz % 4, :, y])
@@ -152,32 +155,35 @@
         lambda yy: bbuf.at[yy, pl.ds(32, 32)],
     )
 
+    ld_b.wait()
+    ring_r.start()
     ld_a.wait()
     line_r.hop(1)
-    ld_b.wait()
-    ring_r.start()
     for d in (1, 7, 2, 6, 3, 5, 4):
         arrive(gbuf.at[p, (z + 8 - d) % 8, y], asem[d])
-    ring_p.start()
+    for ring in rings_p:
+        ring.start()
     line_g.hop(1)
     line_r.hop(2)
-    ring_r.forward()
     line_r.hop(3)
     line_g.hop(2)
-    ring_p.forward()
+    rings_p[0].forward()
+    rings_p[1].forward()
+    ring_r.forward()
     line_r.hop(4)
     line_g.hop(3)
-    ring_p.finish()
-
-    lbuf[p] = jnp.dot(
-        abuf[...].reshape(256, 1024), gbuf[p].reshape(1024, 256), preferred_element_type=F32
-    ).astype(BF16)
-    psem = [new_recv() for _ in range(4)]
-    for d in (1, 3, 2):
-        send(lbuf.at[p], lbuf.at[p], fdev(4 * g + (p + d) % 4, y), psem[d])
+
+    psem = [[new_recv() for _ in range(4)] for _ in range(2)]
+    for h, lanes in enumerate(halves):
+        rings_p[h].finish()
+        lbuf[p, h] = jnp.dot(
+            abuf[...].reshape(256, 1024), gbuf[p, :, :, :, lanes].reshape(1024, 128), preferred_element_type=F32
+        ).astype(BF16)
+        for d in (1, 3, 2):
+            send(lbuf.at[p, h], lbuf.at[p, h], fdev(4 * g + (p + d) % 4, y), psem[h][d])
+    rings[0].start()
     line_g.hop(4)
-    for ring in rings:
-        ring.start()
+    rings[1].start()
 
     def add_squares(t, total):
         part = gbuf[p, t].reshape(128, 256).astype(F32)
@@ -206,15 +212,16 @@
     statistics(p)
     ring_r.finish()
 
-    def tile_part(s):
-        cols = pl.ds(pl.multiple_of(256 * s, 256), 256)
-        return lax.dot_general(lbuf[s], bbuf[:, :, cols].reshape(256, 256), NT, preferred_element_type=F32)
-
-    prod = tile_part(p)
-    for d in (1, 3, 2):
-        s = (p + 4 - d) % 4
-        arrive(lbuf.at[s], psem[d])
-        prod = prod + tile_part(s)
+    def tile_part(s, h):
+        cols = pl.ds(pl.multiple_of(256 * s + 128 * h, 128), 128)
+        return lax.dot_general(lbuf[s, h], bbuf[:, :, cols].reshape(256, 128), NT, preferred_element_type=F32)
+
+    prod = tile_part(p, 0) + tile_part(p, 1)
+    for h in range(2):
+        for d in (1, 3, 2):
+            s = (p + 4 - d) % 4
+            arrive(lbuf.at[s, h], psem[h][d])
+            prod = prod + tile_part(s, h)
     pbuf[...] = prod.astype(BF16).reshape(4, 2, 32, 256)
 
     mycols = pl.ds(pl.multiple_of(256 * p, 256), 256)
@@ -222,7 +229,7 @@
         for j in range(2):
             k, hz, hy = 2 * q + j, 2 * q + y // 2, 2 * (y % 2) + j
             itself = (hz == z) & (hy == y)
-            src, place, arrival = pbuf.at[q, j], home.at[g, :, mycols], hsem.at[4 * g + p]
+            src, place, arrival = pbuf.at[q, j], land.at[r, g, :, mycols], hsem.at[4 * g + p]
             away = pltpu.make_async_remote_copy(
                 src_ref=src, dst_ref=place, send_sem=hsend.at[k], recv_sem=arrival,
                 device_id=fdev(hz, hy), device_id_type=MESH,
@@ -231,84 +238,115 @@
             pl.when(itself)(here.start)
             pl.when(jnp.logical_not(itself))(away.start)
             pending.append((away, jnp.logical_not(itself)))
+
     squares = jnp.sum(jnp.sum(prod * prod, axis=0, keepdims=True), axis=1, keepdims=True)
     row = lax.broadcasted_iota(jnp.int32, (8, 128), 0)
-    sums[f] = jnp.where(row < 4, squares, grad_squares)
+    sum_y[y] = jnp.where(row < 4, squares, grad_squares)
+    ysem = [new_recv() for _ in range(4)]
+    for d in (2, 1, 3):
+        send(sum_y.at[y], sum_y.at[y], fdev(z, (y + d) % 4), ysem[d])
+    rings[0].forward()
+    bsem = [new_recv() for _ in range(4)]
+    for d in range(1, 4):
+        strip = gbuf.at[p, :, (y + d) % 4]
+        send(strip, strip, fdev(4 * g + beside, y), bsem[d])
+    for d in (1, 3, 2):
+        arrive(sum_y.at[(y + 4 - d) % 4], ysem[d])
+    sum_z[z] = sum_y[0] + sum_y[1] + sum_y[2] + sum_y[3]
+    zsem = [new_recv() for _ in range(8)]
+    for d in (4, 3, 5, 2, 6, 1, 7):
+        send(sum_z.at[z], sum_z.at[z], fdev((z + d) % 8, y), zsem[d])
+
+    order = (g, 1 - g)
+
+    def rep_of(q, dx):
+        return ((x + dx + 4) % 4) * 4 + (yl + q - 2 * yl * q) * 2 + c
+
+    sib_waits = []
+
+    def share(rr, k):
+        sem = new_recv()
+        ref = land.at[rr, order[k]]
+        send(ref, ref, sib, sem)
+        sib_waits.append((rr + 1 - 2 * c, k, sem))
+
+    y_sem = [new_recv() for _ in range(2)]
+    xsem = [[[new_recv() for _ in range(2)] for _ in range(4)] for _ in range(2)]
+    for k in range(2):
+        for q in range(4):
+            arrive(land.at[r, order[k], :, pl.ds(256 * q, 256)], hsem.at[4 * order[k] + q])
+        mine = land.at[r, order[k]]
+        send(mine, mine, ylo, y_sem[k])
+        for d in (1, 3, 2):
+            send(mine, mine, {"rep": rep_of(0, d)}, xsem[0][d][k])
+        share(r, k)
+    for k in range(2):
+        mine = land.at[r_ylo, order[k]]
+        arrive(mine, y_sem[k])
+        for d in (1, 3, 2):
+            send(mine, mine, {"rep": rep_of(0, d)}, xsem[1][d][k])
+        share(r_ylo, k)
+
+    for d in (1, 7, 2, 6, 3, 5, 4):
+        arrive(sum_z.at[(z + 8 - d) % 8], zsem[d])
+    for q in range(2):
+        total = sum_z[4 * q] + sum_z[4 * q + 1] + sum_z[4 * q + 2] + sum_z[4 * q + 3]
+        norm = jnp.sqrt(total[4:5, 0:1]) / jnp.sqrt(total[0:1, 0:1] + EPSILON)
+        ratio[r, q] = jnp.broadcast_to(norm, (8, 128))
 
     def tell(d, _):
         pltpu.make_async_remote_copy(
-            src_ref=sums.at[f], dst_ref=sums.at[f], send_sem=zsem.at[0], recv_sem=zsem.at[1],
-            device_id={"fsdp": (f + d) % 32}, device_id_type=MESH,
+            src_ref=ratio.at[r], dst_ref=ratio.at[r], send_sem=tsem.at[0], recv_sem=tsem.at[1],
+            device_id={"rep": (r + d) % 16}, device_id_type=MESH,
         ).start()
         return 0
 
-    lax.fori_loop(1, 32, tell, 0)
-    rings[0].forward()
-
-    for k in range(8):
-        arrive(home.at[k // 4, :, pl.ds(256 * (k % 4), 256)], hsem.at[k])
-    everyone = pltpu.make_async_remote_copy(
-        src_ref=sums.at[pl.ds(0, 31)], dst_ref=sums.at[pl.ds(0, 31)], send_sem=zsem.at[0], recv_sem=zsem.at[1],
+    lax.fori_loop(1, 16, tell, 0)
+    rings[1].forward()
+    for d in (1, 2, 3):
+        arrive(gbuf.at[beside, :, (y + d) % 4], bsem[d])
+    statistics(beside)
+    for d in (1, 3, 2):
+        for k in range(2):
+            arrive(land.at[rep_of(0, -d), order[k]], xsem[0][d][k])
+            share(rep_of(0, -d), k)
+    rings[0].finish()
+    statistics(others[0])
+    told = pltpu.make_async_remote_copy(
+        src_ref=ratio.at[pl.ds(0, 15)], dst_ref=ratio.at[pl.ds(0, 15)], send_sem=tsem.at[0], recv_sem=tsem.at[1],
         device_id=north, device_id_type=MESH,
     )
-    everyone.wait_recv()
-    done = []
-    for q in range(2):
-        total = jnp.sum(sums[16 * q:16 * q + 16], axis=0)
-        ratio = jnp.sqrt(total[4:5, 0:1]) / jnp.sqrt(total[0:1, 0:1] + EPSILON)
-        done.append((home[q].astype(F32) * ratio).astype(BF16))
-    own[:, 0:1024] = jnp.where(swap, done[1], done[0])
-    own[:, 1024:2048] = jnp.where(swap, done[0], done[1])
-
-    def slot(rr):
-        return upd.at[:, pl.ds(pl.multiple_of(rr * 2048, 2048), 2048)]
-
-    sib_waits = []
-
-    def share(rr, src=None):
-        sem = new_recv()
-        send(slot(rr) if src is None else src, slot(rr), sib, sem)
-        sib_waits.append((slot(rr + 1 - 2 * c), sem))
-
-    def rep_of(q, dx):
-        return ((x + dx + 4) % 4) * 4 + (yl + q - 2 * yl * q) * 2 + c
-
-    y_sem = new_recv()
-    xsem = [[new_recv() for _ in range(4)] for _ in range(2)]
-    send(own, slot(r), ylo, y_sem)
+    told.wait_recv()
+
+    def emit(rr):
+        swapped = table[0, rr] != 0
+        scaled = [(land[rr, q].astype(F32) * ratio[rr, q, 0:1, 0:1]).astype(BF16) for q in range(2)]
+        for k in range(2):
+            cols = pl.ds(pl.multiple_of(rr * 2048 + 1024 * k, 1024), 1024)
+            upd[:, cols] = jnp.where(swapped, scaled[1 - k], scaled[k])
+
+    emit(r)
+    emit(r_ylo)
     for d in (1, 3, 2):
-        send(own, slot(r), {"rep": rep_of(0, d)}, xsem[0][d])
-    share(r, own)
-    keep = pltpu.make_async_copy(own, slot(r), lsem.at[0])
-    keep.start()
-    rings[1].forward()
-    arrive(slot(r_ylo), y_sem)
+        emit(rep_of(0, -d))
     for d in (1, 3, 2):
-        send(slot(r_ylo), slot(r_ylo), {"rep": rep_of(0, d)}, xsem[1][d])
-    share(r_ylo)
-    rings[2].forward()
-    for q in range(2):
-        for d in (1, 3, 2):
-            arrive(slot(rep_of(q, -d)), xsem[q][d])
-            share(rep_of(q, -d))
-    for ring, s in zip(rings, others):
-        ring.finish()
-        statistics(s)
-    st_l = pltpu.make_async_copy(lf, left_out.at[0], lsem.at[3])
-    st_l.start()
-    st_r = pltpu.make_async_copy(rf, right_out.at[0], lsem.at[4])
-    st_r.start()
-    for ref, sem in sib_waits:
-        arrive(ref, sem)
+        for k in range(2):
+            arrive(land.at[rep_of(1, -d), order[k]], xsem[1][d][k])
+            share(rep_of(1, -d), k)
+    rings[1].finish()
+    statistics(others[1])
+    for d in (1, 3, 2):
+        emit(rep_of(1, -d))
+    for rr, k, sem in sib_waits:
+        arrive(land.at[rr, order[k]], sem)
+        if k == 1:
+            emit(rr)
     for copy, pred in pending:
         if pred is None:
             copy.wait_send()
         else:
             pl.when(pred)(copy.wait_send)
-    everyone.wait_send()
-    keep.wait()
-    st_l.wait()
-    st_r.wait()
+    told.wait_send()
 
 
 def pinned(array):
@@ -317,7 +355,6 @@
 
 def body(gradient, owner_table, left_factor, right_factor, left_root, right_root):
     vmem = pltpu.VMEM
-    anywhere = pl.BlockSpec(memory_space=pl.ANY)
     hbm = pl.BlockSpec(memory_space=pltpu.HBM)
     return pl.pallas_call(
         kernel,
@@ -327,7 +364,7 @@
             vmem((1, 64, 1024), F32),
         ),
         in_specs=[hbm] * 6,
-        out_specs=(anywhere,) * 3,
+        out_specs=(pl.BlockSpec(memory_space=pltpu.VMEM),) * 3,
         scratch_shapes=[
             pltpu.SMEM((2, 16), jnp.int32),
             vmem((32, 2048), BF16),
@@ -335,17 +372,16 @@
             vmem((4, 8, 4, 32, 256), BF16),
             vmem((4, 64, 1024), BF16),
             vmem((4, 64, 1024), BF16),
-            vmem((4, 256, 256), BF16),
+            vmem((4, 2, 256, 128), BF16),
             vmem((4, 2, 32, 256), BF16),
-            vmem((2, 32, 1024), BF16),
-            vmem((32, 2048), BF16),
-            vmem((64, 1024), F32),
-            vmem((64, 1024), F32),
+            vmem((16, 2, 32, 1024), BF16),
             vmem((128, 256), F32),
-            vmem((32, 8, 128), F32),
+            vmem((4, 8, 128), F32),
+            vmem((8, 8, 128), F32),
+            vmem((16, 2, 8, 128), F32),
             pltpu.SemaphoreType.DMA((6,)),
-            pltpu.SemaphoreType.DMA((80,)),
-            pltpu.SemaphoreType.DMA((80,)),
+            pltpu.SemaphoreType.DMA((112,)),
+            pltpu.SemaphoreType.DMA((112,)),
             pltpu.SemaphoreType.DMA((8,)),
             pltpu.SemaphoreType.DMA((2,)),
             pltpu.SemaphoreType.DMA((8,)),

time: 87.1 us -> 77.6 us (0.89)
  Pallas kernels: 83.6 us -> 74.1 us
    pallas_call x1, Pallas kernels: 83.6 us -> 74.1 us  [body(): pl.pallas_call(kernel, out_shape=(vmem((32, 32768), BF16), vmem((1, 64, 1...]
where the time goes in v3:
time: 77.6 us; the launch traced here: 77.4 us
  Pallas kernels  74.1 us (95%)
  local copies, waits for them, and re-layouts  2.73 us (4%)
    pallas_call x1, Pallas kernels, body(): pl.pallas_call(kernel, out_shape=(vmem((32, 32768), BF16), vmem((1, 64, 1...  74.1 us
    unnamed x3, local copies, waits for them, and re-layouts  2.73 us

profile of v3, /device:TPU:1, one launch (start us, length us, event | category | flops | bytes accessed | tf_op | source)
XLA Modules:
  0.0 77.4 jit_solution(6416541098507015375)
XLA Ops:
  0.6 74.1 %shard_map.85 = (bf16[32,32768]{1,0:T(8,128)(2,1)S(1)}, f32[1,64,1024]{2,1,0:T(8,128)S(1)}, f32[1,64,1024]{2,1,0:T(8,128)S(1)}) custom-call(bf16[32,2048]{1,0:T(8,128)(2,1)} %grad_in.1, s32[2,16]{1,0:T(2,128)} %bitcast.1, f32[1,64,1024]{2,1,0:T(8,128)} %lf_in.1, f32[1,64,1024]{2,1,0:T(8,128)} %rf_in.1, bf16[1,64,1024]{2,1,0:T(8,128)(2,1)} %lr_in.1, ...), custom_call_target="tpu_custom_call" | custom-call | tf_op jit(solution)/shard_map/pallas_call | solution.py:359
  74.7 1.3 %copy.12 = bf16[32,32768]{1,0:T(8,128)(2,1)} copy(bf16[32,32768]{1,0:T(8,128)(2,1)S(1)} %get-tuple-element.3) | data formatting | bytes 4194304
  76.0 0.7 copy.13
  76.7 0.7 copy.14

commit v4 on v3

--- a/solution.py
+++ b/solution.py
@@ -30,6 +30,7 @@
         return {"fsdp": zz * 4 + yy}
 
     up, down, north, south = fdev((z + 1) % 8, y), fdev((z + 7) % 8, y), fdev(z, yn), fdev(z, yp)
+    up2, down2 = fdev((z + 2) % 8, y), fdev((z + 6) % 8, y)
     r_sib, r_ylo = r + 1 - 2 * c, r + 2 - 4 * yl
     sib, ylo = {"rep": r_sib}, {"rep": r_ylo}
 
@@ -84,20 +85,33 @@
     class Line:
         def __init__(self, slot):
             self.slot = slot
-            self.plus = [None] + [new_recv() for _ in range(3)]
-            self.minus = [None] + [new_recv() for _ in range(3)]
-
-        def hop(self, d):
-            if d >= 2:
-                arrive(self.slot(jnp.maximum(z - d + 1, 0)), self.plus[d - 1], p >= d - 1)
-            if d <= 3:
-                src = self.slot(jnp.maximum(z - d + 1, 0))
-                send(src, src, up, self.plus[d], (p >= d - 1) & (p <= 2))
-            if d >= 2:
-                arrive(self.slot(jnp.minimum(z + d - 1, 7)), self.minus[d - 1], p <= 4 - d)
-            if d <= 3:
-                src = self.slot(jnp.minimum(z + d - 1, 7))
-                send(src, src, down, self.minus[d], (p <= 4 - d) & (p >= 1))
+            self.plus = [new_recv() for _ in range(4)]
+            self.minus = [new_recv() for _ in range(4)]
+
+        def below(self, d):
+            return self.slot(jnp.maximum(z - d, 0))
+
+        def above(self, d):
+            return self.slot(jnp.minimum(z + d, 7))
+
+        def start(self):
+            mine = self.slot(z)
+            send(mine, mine, up2, self.plus[2], p <= 1)
+            send(mine, mine, down2, self.minus[2], p >= 2)
+            send(mine, mine, up, self.plus[1], p <= 2)
+            send(mine, mine, down, self.minus[1], p >= 1)
+
+        def forward(self):
+            arrive(self.below(2), self.plus[2], p >= 2)
+            send(self.below(2), self.below(2), up, self.plus[3], p == 2)
+            arrive(self.above(2), self.minus[2], p <= 1)
+            send(self.above(2), self.above(2), down, self.minus[3], p == 1)
+
+        def finish(self):
+            arrive(self.below(1), self.plus[1], p >= 1)
+            arrive(self.above(1), self.minus[1], p <= 2)
+            arrive(self.below(3), self.plus[3], p == 3)
+            arrive(self.above(3), self.minus[3], p == 0)
 
     class Ring:
         def __init__(self, slot, first, second):
@@ -158,38 +172,36 @@
     ld_b.wait()
     ring_r.start()
     ld_a.wait()
-    line_r.hop(1)
+    line_r.start()
     for d in (1, 7, 2, 6, 3, 5, 4):
         arrive(gbuf.at[p, (z + 8 - d) % 8, y], asem[d])
     for ring in rings_p:
         ring.start()
-    line_g.hop(1)
-    line_r.hop(2)
-    line_r.hop(3)
-    line_g.hop(2)
+    line_g.start()
+    line_r.forward()
     rings_p[0].forward()
     rings_p[1].forward()
     ring_r.forward()
-    line_r.hop(4)
-    line_g.hop(3)
-
-    psem = [[new_recv() for _ in range(4)] for _ in range(2)]
+    line_g.forward()
+    rings[0].start()
+    line_r.finish()
+
+    lines_l = [Line(lambda zz, h=h: lbuf.at[zz % 4, h]) for h in range(2)]
     for h, lanes in enumerate(halves):
         rings_p[h].finish()
         lbuf[p, h] = jnp.dot(
             abuf[...].reshape(256, 1024), gbuf[p, :, :, :, lanes].reshape(1024, 128), preferred_element_type=F32
         ).astype(BF16)
-        for d in (1, 3, 2):
-            send(lbuf.at[p, h], lbuf.at[p, h], fdev(4 * g + (p + d) % 4, y), psem[h][d])
-    rings[0].start()
-    line_g.hop(4)
-    rings[1].start()
+        lines_l[h].start()
+    lines_l[0].forward()
 
     def add_squares(t, total):
         part = gbuf[p, t].reshape(128, 256).astype(F32)
         return total + jnp.sum(part * part, axis=0, keepdims=True)
 
     grad_squares = lax.fori_loop(0, 8, add_squares, jnp.zeros((1, 256), F32))
+    lines_l[1].forward()
+    line_g.finish()
     grad_squares = 0.25 * jnp.sum(grad_squares, axis=1, keepdims=True)
 
     scale = (1.0 - BETA) / 1024
@@ -211,6 +223,7 @@
     lf[...] = BETA * lf[...]
     statistics(p)
     ring_r.finish()
+    rings[0].forward()
 
     def tile_part(s, h):
         cols = pl.ds(pl.multiple_of(256 * s + 128 * h, 128), 128)
@@ -218,10 +231,9 @@
 
     prod = tile_part(p, 0) + tile_part(p, 1)
     for h in range(2):
-        for d in (1, 3, 2):
-            s = (p + 4 - d) % 4
-            arrive(lbuf.at[s, h], psem[h][d])
-            prod = prod + tile_part(s, h)
+        lines_l[h].finish()
+        for d in range(1, 4):
+            prod = prod + tile_part((p + d) % 4, h)
     pbuf[...] = prod.astype(BF16).reshape(4, 2, 32, 256)
 
     mycols = pl.ds(pl.multiple_of(256 * p, 256), 256)
@@ -245,11 +257,6 @@
     ysem = [new_recv() for _ in range(4)]
     for d in (2, 1, 3):
         send(sum_y.at[y], sum_y.at[y], fdev(z, (y + d) % 4), ysem[d])
-    rings[0].forward()
-    bsem = [new_recv() for _ in range(4)]
-    for d in range(1, 4):
-        strip = gbuf.at[p, :, (y + d) % 4]
-        send(strip, strip, fdev(4 * g + beside, y), bsem[d])
     for d in (1, 3, 2):
         arrive(sum_y.at[(y + 4 - d) % 4], ysem[d])
     sum_z[z] = sum_y[0] + sum_y[1] + sum_y[2] + sum_y[3]
@@ -277,15 +284,24 @@
             arrive(land.at[r, order[k], :, pl.ds(256 * q, 256)], hsem.at[4 * order[k] + q])
         mine = land.at[r, order[k]]
         send(mine, mine, ylo, y_sem[k])
-        for d in (1, 3, 2):
+        for d in (2, 1, 3):
             send(mine, mine, {"rep": rep_of(0, d)}, xsem[0][d][k])
         share(r, k)
+    rings[1].start()
+    bsem = [new_recv() for _ in range(4)]
+    for d in range(1, 4):
+        strip = gbuf.at[p, :, (y + d) % 4]
+        send(strip, strip, fdev(4 * g + beside, y), bsem[d])
     for k in range(2):
         mine = land.at[r_ylo, order[k]]
         arrive(mine, y_sem[k])
-        for d in (1, 3, 2):
+        for d in (2, 1, 3):
             send(mine, mine, {"rep": rep_of(0, d)}, xsem[1][d][k])
         share(r_ylo, k)
+    for k in range(2):
+        across = land.at[rep_of(0, 2), order[k]]
+        arrive(across, xsem[0][2][k])
+        share(rep_of(0, 2), k)
 
     for d in (1, 7, 2, 6, 3, 5, 4):
         arrive(sum_z.at[(z + 8 - d) % 8], zsem[d])
@@ -303,10 +319,7 @@
 
     lax.fori_loop(1, 16, tell, 0)
     rings[1].forward()
-    for d in (1, 2, 3):
-        arrive(gbuf.at[beside, :, (y + d) % 4], bsem[d])
-    statistics(beside)
-    for d in (1, 3, 2):
+    for d in (1, 3):
         for k in range(2):
             arrive(land.at[rep_of(0, -d), order[k]], xsem[0][d][k])
             share(rep_of(0, -d), k)
@@ -333,6 +346,9 @@
         for k in range(2):
             arrive(land.at[rep_of(1, -d), order[k]], xsem[1][d][k])
             share(rep_of(1, -d), k)
+    for d in (1, 2, 3):
+        arrive(gbuf.at[beside, :, (y + d) % 4], bsem[d])
+    statistics(beside)
     rings[1].finish()
     statistics(others[1])
     for d in (1, 3, 2):
@@ -349,6 +365,16 @@
     told.wait_send()
 
 
+def deliver(upd, left, right, upd_out, left_out, right_out, sem):
+    pairs = [(upd.at[pl.ds(16 * k, 16)], upd_out.at[pl.ds(16 * k, 16)]) for k in range(2)]
+    pairs += [(left, left_out), (right, right_out)]
+    copies = [pltpu.make_async_copy(src, dst, sem.at[k]) for k, (src, dst) in enumerate(pairs)]
+    for copy in copies:
+        copy.start()
+    for copy in copies:
+        copy.wait()
+
+
 def pinned(array):
     return pltpu.with_memory_space_constraint(array, pltpu.HBM)
 
@@ -356,7 +382,7 @@
 def body(gradient, owner_table, left_factor, right_factor, left_root, right_root):
     vmem = pltpu.VMEM
     hbm = pl.BlockSpec(memory_space=pltpu.HBM)
-    return pl.pallas_call(
+    results = pl.pallas_call(
         kernel,
         out_shape=(
             vmem((32, 32768), BF16),
@@ -393,6 +419,14 @@
         pinned(gradient), pinned(owner_table.T), pinned(left_factor), pinned(right_factor),
         pinned(left_root), pinned(right_root),
     )
+    return pl.pallas_call(
+        deliver,
+        out_shape=tuple(pltpu.HBM(a.shape, a.dtype) for a in results),
+        in_specs=[pl.BlockSpec(memory_space=pltpu.VMEM)] * 3,
+        out_specs=(hbm,) * 3,
+        scratch_shapes=[pltpu.SemaphoreType.DMA((6,))],
+        compiler_params=pltpu.CompilerParams(vmem_limit_bytes=40 * 1024 * 1024),
+    )(*[pltpu.with_memory_space_constraint(a, pltpu.VMEM) for a in results])
 
 
 def solution(mesh):

time: 77.6 us -> 74.1 us (0.955)
  local copies, waits for them, and re-layouts: 2.73 us -> 0 us
  Pallas kernels: 74.1 us -> 73.3 us
    unnamed x3 -> x0, local copies, waits for them, and re-layouts: 2.73 us -> none
    pallas_call x1, Pallas kernels: 74.1 us -> 71.8 us  [body(): pl.pallas_call(kernel, out_shape=(vmem((32, 32768), BF16), vmem((1, 64, 1...]
    pallas_call x0 -> x1, Pallas kernels: none -> 1.54 us  [body(): pl.pallas_call(deliver, out_shape=tuple((pltpu.HBM(a.shape, a.dtype) for...]
where the time goes in v4:
time: 74.1 us; the launch traced here: 74 us
  Pallas kernels  73.3 us (99%)
    pallas_call x1, Pallas kernels, body(): pl.pallas_call(kernel, out_shape=(vmem((32, 32768), BF16), vmem((1, 64, 1...  71.8 us
    pallas_call x1, Pallas kernels, body(): pl.pallas_call(deliver, out_shape=tuple((pltpu.HBM(a.shape, a.dtype) for...  1.54 us

profile of v4, /device:TPU:1, one launch (start us, length us, event | category | flops | bytes accessed | tf_op | source)
XLA Modules:
  0.0 74.0 jit_solution(8604725509837404301)
XLA Ops:
  0.6 71.8 %shard_map.85 = (bf16[32,32768]{1,0:T(8,128)(2,1)S(1)}, f32[1,64,1024]{2,1,0:T(8,128)S(1)}, f32[1,64,1024]{2,1,0:T(8,128)S(1)}) custom-call(bf16[32,2048]{1,0:T(8,128)(2,1)} %grad_in.1, s32[2,16]{1,0:T(2,128)} %bitcast.1, f32[1,64,1024]{2,1,0:T(8,128)} %lf_in.1, f32[1,64,1024]{2,1,0:T(8,128)} %rf_in.1, bf16[1,64,1024]{2,1,0:T(8,128)(2,1)} %lr_in.1, ...), custom_call_target="tpu_custom_call" | custom-call | tf_op jit(solution)/shard_map/pallas_call | solution.py:385
  72.4 1.5 %shard_map.86 = (bf16[32,32768]{1,0:T(8,128)(2,1)}, f32[1,64,1024]{2,1,0:T(8,128)}, f32[1,64,1024]{2,1,0:T(8,128)}) custom-call(bf16[32,32768]{1,0:T(8,128)(2,1)S(1)} %get-tuple-element.6.upd, f32[1,64,1024]{2,1,0:T(8,128)S(1)} %get-tuple-element.7.left, f32[1,64,1024]{2,1,0:T(8,128)S(1)} %get-tuple-element.8.right), custom_call_target="tpu_custom_call" | custom-call | tf_op jit(solution)/shard_map/pallas_call | solution.py:422

commit v5 on v4

--- a/solution.py
+++ b/solution.py
@@ -162,7 +162,8 @@
     others = [(p + 2) % 4, 3 - p]
     rings = [ring_of(s) for s in others]
     line_r = Line(lambda zz: abuf.at[zz % 4])
-    line_g = Line(lambda zz: gbuf.at[zz % 4, :, y])
+    cross = [new_recv() for _ in range(2)]
+    far, last = gbuf.at[others[0], :, y], gbuf.at[others[1], :, y]
     ring_r = Ring(
         lambda yy: bbuf.at[yy],
         lambda yy: bbuf.at[yy, pl.ds(0, 32)],
@@ -177,12 +178,12 @@
         arrive(gbuf.at[p, (z + 8 - d) % 8, y], asem[d])
     for ring in rings_p:
         ring.start()
-    line_g.start()
+    send(gbuf.at[p, :, y], gbuf.at[p, :, y], fdev(4 * g + others[0], y), cross[0])
     line_r.forward()
     rings_p[0].forward()
     rings_p[1].forward()
     ring_r.forward()
-    line_g.forward()
+    arrive(far, cross[0])
     rings[0].start()
     line_r.finish()
 
@@ -201,7 +202,7 @@
 
     grad_squares = lax.fori_loop(0, 8, add_squares, jnp.zeros((1, 256), F32))
     lines_l[1].forward()
-    line_g.finish()
+    send(far, far, fdev(4 * g + beside, y), cross[1])
     grad_squares = 0.25 * jnp.sum(grad_squares, axis=1, keepdims=True)
 
     scale = (1.0 - BETA) / 1024
@@ -264,6 +265,9 @@
     for d in (4, 3, 5, 2, 6, 1, 7):
         send(sum_z.at[z], sum_z.at[z], fdev((z + d) % 8, y), zsem[d])
 
+    arrive(last, cross[1])
+    rings[1].start()
+
     order = (g, 1 - g)
 
     def rep_of(q, dx):
@@ -287,9 +291,8 @@
         for d in (2, 1, 3):
             send(mine, mine, {"rep": rep_of(0, d)}, xsem[0][d][k])
         share(r, k)
-    rings[1].start()
     bsem = [new_recv() for _ in range(4)]
-    for d in range(1, 4):
+    for d in range(4):
         strip = gbuf.at[p, :, (y + d) % 4]
         send(strip, strip, fdev(4 * g + beside, y), bsem[d])
     for k in range(2):
@@ -303,6 +306,8 @@
         arrive(across, xsem[0][2][k])
         share(rep_of(0, 2), k)
 
+    rings[1].forward()
+
     for d in (1, 7, 2, 6, 3, 5, 4):
         arrive(sum_z.at[(z + 8 - d) % 8], zsem[d])
     for q in range(2):
@@ -318,7 +323,6 @@
         return 0
 
     lax.fori_loop(1, 16, tell, 0)
-    rings[1].forward()
     for d in (1, 3):
         for k in range(2):
             arrive(land.at[rep_of(0, -d), order[k]], xsem[0][d][k])
@@ -346,7 +350,7 @@
         for k in range(2):
             arrive(land.at[rep_of(1, -d), order[k]], xsem[1][d][k])
             share(rep_of(1, -d), k)
-    for d in (1, 2, 3):
+    for d in range(4):
         arrive(gbuf.at[beside, :, (y + d) % 4], bsem[d])
     statistics(beside)
     rings[1].finish()

time: 74.1 us -> 73.7 us (level)
  no operation moved by 1% of the time
where the time goes in v5:
time: 73.7 us; the launch traced here: 73.6 us
  Pallas kernels  72.9 us (99%)
    pallas_call x1, Pallas kernels, body(): pl.pallas_call(kernel, out_shape=(vmem((32, 32768), BF16), vmem((1, 64, 1...  71.4 us
    pallas_call x1, Pallas kernels, body(): pl.pallas_call(deliver, out_shape=tuple((pltpu.HBM(a.shape, a.dtype) for...  1.54 us

profile of v5, /device:TPU:1, one launch (start us, length us, event | category | flops | bytes accessed | tf_op | source)
XLA Modules:
  0.0 73.6 jit_solution(9483973760992379446)
XLA Ops:
  0.6 71.4 %shard_map.85 = (bf16[32,32768]{1,0:T(8,128)(2,1)S(1)}, f32[1,64,1024]{2,1,0:T(8,128)S(1)}, f32[1,64,1024]{2,1,0:T(8,128)S(1)}) custom-call(bf16[32,2048]{1,0:T(8,128)(2,1)} %grad_in.1, s32[2,16]{1,0:T(2,128)} %bitcast.1, f32[1,64,1024]{2,1,0:T(8,128)} %lf_in.1, f32[1,64,1024]{2,1,0:T(8,128)} %rf_in.1, bf16[1,64,1024]{2,1,0:T(8,128)(2,1)} %lr_in.1, ...), custom_call_target="tpu_custom_call" | custom-call | tf_op jit(solution)/shard_map/pallas_call | solution.py:389
  72.0 1.5 %shard_map.86 = (bf16[32,32768]{1,0:T(8,128)(2,1)}, f32[1,64,1024]{2,1,0:T(8,128)}, f32[1,64,1024]{2,1,0:T(8,128)}) custom-call(bf16[32,32768]{1,0:T(8,128)(2,1)S(1)} %get-tuple-element.6.upd, f32[1,64,1024]{2,1,0:T(8,128)S(1)} %get-tuple-element.7.left, f32[1,64,1024]{2,1,0:T(8,128)S(1)} %get-tuple-element.8.right), custom_call_target="tpu_custom_call" | custom-call | tf_op jit(solution)/shard_map/pallas_call | solution.py:426
